TPU v7x, 512 devices: a whole 4x4x16 slice. The times are simulated.
512 devices in a mesh: section: 16 (over z), node: 32 (over y, x, core).
Axes of the slice: x: 4, y: 4, z: 16, core: 2. Of those that a mesh axis runs over, the one named last changes fastest.
Arguments:
- initial: bfloat16 [2, 16384, 256], P(None, 'node'), may hold values from -6 to 6
- adjacency: bfloat16 [2, 384, 128, 128], P(None, 'node'), may hold values from -0.5 to 0.5
- sources: int32 [2, 384], P(None, 'node'), may hold values from 0 to 5, as said below
- boundary_rows: int32 [2, 4096], P(None, 'node'), may hold values from 0 to 511, as said below
- boundary_count: int32 [2, 32], P(None, 'node'), may hold values from 32 to 128, as said below
- layer_weights: bfloat16 [16, 256, 256], P('section'), may hold values from -0.375 to 0.375
Outputs:
- section_out: bfloat16 [16, 2, 16384, 256], P('section', None, 'node')
Inputs may be any that keep to these rules, and one draw needn't show every extreme that they name: `sources`: each aligned group of 3 entries names, in some order, one of the partition's own tiles 0 .. 3, tile 512 // 128 (the previous partition's boundary block) and tile 512 // 128 + 1 (the next one's). `boundary_rows`: the 128 entries of one partition are distinct rows of it. `boundary_count`: some partition of each span has a full block.
All inputs are finite; a program needn't handle non-finite values.
Results may differ from a plain program's by a relative error of at most 0.027.
Values may be sent and summed in bfloat16 or wider, within the bound.
A program may use at most 64 MiB of HBM per device.

v0:
```python
import jax
import jax.numpy as jnp
from jax import lax
from jax.sharding import PartitionSpec as P

alpha_mix = 0.1
lambda_decay = 0.5


def extended_2(cells, sides, width):
    for axis, dim in sides:
        count = lax.axis_size(axis)
        head = lax.slice_in_dim(cells, 0, width, axis=dim)
        tail = lax.slice_in_dim(cells, cells.shape[dim] - width, cells.shape[dim], axis=dim)
        cells = jnp.concatenate(
            [
                lax.ppermute(tail, axis, [(i, (i + 1) % count) for i in range(count)]),
                cells,
                lax.ppermute(head, axis, [((i + 1) % count, i) for i in range(count)]),
            ],
            axis=dim,
        )
    return cells


def from_behind(x, axis, by):
    size = lax.axis_size(axis)
    pairs = [(i, i + by) for i in range(size) if 0 <= i + by < size]
    return lax.ppermute(x, axis, pairs)


def build_pool(hidden, boundary_rows, boundary_count, tile_size):
    count_spans, row_count, width = hidden.shape
    rim_size = boundary_rows.shape[1]
    live_mask = (jnp.arange(rim_size)[None, :] < boundary_count).astype(jnp.bfloat16)
    rim_rows = (
        jnp.take_along_axis(hidden, boundary_rows[:, :, None], axis=1) * live_mask[:, :, None]
    )
    extended = extended_2(rim_rows, (("node", 1),), rim_size)
    preceding = extended[:, :rim_size]
    following = extended[:, 2 * rim_size :]
    source_pool = jnp.concatenate([hidden, preceding, following], axis=1)
    return source_pool.reshape(count_spans, -1, tile_size, width)


def finish_rows(aggregate, anchor, weight, mixing):
    count_spans, row_count, width = aggregate.shape
    blended = (1.0 - alpha_mix) * aggregate + alpha_mix * anchor.astype(jnp.float32)
    blended_b = blended.astype(jnp.bfloat16).reshape(count_spans * row_count, width)
    projected = jnp.dot(blended_b, weight, preferred_element_type=jnp.float32).reshape(
        count_spans, row_count, width
    )
    return jax.nn.relu((1.0 - mixing) * blended + mixing * projected).astype(jnp.bfloat16)


def gcn_layer(hidden, anchor, adjacency, sources, boundary_rows, boundary_count, weight, mixing):
    count_spans, row_count, width = hidden.shape
    tile_size = adjacency.shape[2]
    source_pool = build_pool(hidden, boundary_rows, boundary_count, tile_size)
    picked = jnp.take_along_axis(source_pool, sources[:, :, None, None], axis=1)
    products = jnp.einsum("cntk,cnkd->cntd", adjacency, picked, preferred_element_type=jnp.float32)
    per_row = products.shape[1] // (row_count // tile_size)
    aggregate = products.reshape(
        count_spans, row_count // tile_size, per_row, tile_size, width
    ).sum(axis=2)
    aggregate = aggregate.reshape(count_spans, row_count, width)
    return finish_rows(aggregate, anchor, weight, mixing)


def run_section(
    hidden, anchor, adjacency, sources, boundary_rows, boundary_count, layer_weights, section_index
):
    layer_number = section_index * layer_weights.shape[0] + 0
    mixing = jnp.log(lambda_decay / (layer_number.astype(jnp.float32) + 1.0) + 1.0)
    hidden = gcn_layer(
        hidden, anchor, adjacency, sources, boundary_rows, boundary_count, layer_weights[0], mixing
    )
    return hidden


def on_device(initial, adjacency, sources, boundary_rows, boundary_count, layer_weights):
    section_index = lax.axis_index("section")
    section_count = lax.axis_size("section")
    section_out = jnp.zeros(initial.shape, jnp.bfloat16)

    def advance(moment, state_pair):
        incoming, collected = state_pair
        hidden = jnp.where(section_index == 0, initial, incoming)
        hidden = run_section(
            hidden,
            initial,
            adjacency,
            sources,
            boundary_rows,
            boundary_count,
            layer_weights,
            section_index,
        )
        collected = jnp.where(moment == section_index, hidden, collected)
        incoming = from_behind(hidden, "section", 1)
        return (incoming, collected)

    state_pair = lax.fori_loop(
        0, section_count, advance, (jnp.zeros(initial.shape, jnp.bfloat16), section_out)
    )
    section_out = state_pair[1]
    return section_out[None]


def solution(mesh):
    in_specs = (
        P(None, "node", None),
        P(None, "node", None, None),
        P(None, "node"),
        P(None, "node"),
        P(None, "node"),
        P("section", None, None),
    )
    out_specs = P("section", None, "node", None)
    return jax.shard_map(
        on_device, mesh=mesh, in_specs=in_specs, out_specs=out_specs, check_vma=False
    )
```

profile of v0, /device:TPU:480, one launch (start us, length us, event | category | flops | bytes accessed | tf_op | source)
XLA Modules:
  0.0 594.7 jit_solution(5306694875906632556)
XLA Ops:
  0.1 594.6 %while.18 = (s32[]{:T(128)}, bf16[2,512,256]{2,1,0:T(8,128)(2,1)S(1)}, bf16[2,512,256]{2,1,0:T(8,128)(2,1)}, f32[]{:T(128)}, s32[2,12]{1,0:T(2,128)}, /*index=5*...) while((s32[]{:T(128)}, ...), condition=%wide.region_2.3_spmd.clone, body=%wide.region_0.2_spmd.clone.sunk | while | flops 343544128 | bytes 48111660 | solution.py:103
  3.5 6.6 %collective-permute-start = (bf16[2,128,256]{2,1,0:T(8,128)(2,1)S(1)}, bf16[2,128,256]{2,1,0:T(8,128)(2,1)S(1)}, u32[]{:S(2)}, u32[]{:S(2)}) collective-permute-start(bf16[2,128,256]{2,1,0:T(8,128)(2,1)S(1)} %select_multiply_fusion.2), channel_id=1, source_target_pairs={{1,0},{2,1},{3,2},{4,3},{5,4},{6,5},{7,6},{8,7},{9,8},{10,9},{11,1... | collective-permute-start | bytes 393224 | tf_op jit(solution)/shard_map/while/body/eval_jaxpr/ppermute | solution.py:19
  13.5 6.1 %collective-permute-done.1 = bf16[2,128,256]{2,1,0:T(8,128)(2,1)S(1)} collective-permute-done((bf16[2,128,256]{2,1,0:T(8,128)(2,1)S(1)}, bf16[2,128,256]{2,1,0:T(8,128)(2,1)S(1)}, u32[]{:S(2)}, u32[]{:S(2)}) %collective-permute-start.1) | collective-permute-done | bytes 131104 | tf_op jit(solution)/shard_map/while/body/eval_jaxpr/ppermute | solution.py:17
  30.7 9.8 %collective-permute-done.2 = bf16[2,512,256]{2,1,0:T(8,128)(2,1)S(1)} collective-permute-done((bf16[2,512,256]{2,1,0:T(8,128)(2,1)S(1)}, bf16[2,512,256]{2,1,0:T(8,128)(2,1)S(1)}, u32[]{:S(2)}, u32[]{:S(2)}) %collective-permute-start.2) | collective-permute-done | bytes 524320 | tf_op jit(solution)/shard_map/while/body/eval_jaxpr/ppermute | solution.py:29
  43.8 4.5 collective-permute-start
  51.7 6.1 %collective-permute-done.1 = bf16[2,128,256]{2,1,0:T(8,128)(2,1)S(1)} collective-permute-done((bf16[2,128,256]{2,1,0:T(8,128)(2,1)S(1)}, bf16[2,128,256]{2,1,0:T(8,128)(2,1)S(1)}, u32[]{:S(2)}, u32[]{:S(2)}) %collective-permute-start.1) | collective-permute-done | bytes 131104 | tf_op jit(solution)/shard_map/while/body/eval_jaxpr/ppermute | solution.py:17
  68.9 9.8 %collective-permute-done.2 = bf16[2,512,256]{2,1,0:T(8,128)(2,1)S(1)} collective-permute-done((bf16[2,512,256]{2,1,0:T(8,128)(2,1)S(1)}, bf16[2,512,256]{2,1,0:T(8,128)(2,1)S(1)}, u32[]{:S(2)}, u32[]{:S(2)}) %collective-permute-start.2) | collective-permute-done | bytes 524320 | tf_op jit(solution)/shard_map/while/body/eval_jaxpr/ppermute | solution.py:29
  82.0 3.0 collective-permute-start
  88.5 6.1 %collective-permute-done.1 = bf16[2,128,256]{2,1,0:T(8,128)(2,1)S(1)} collective-permute-done((bf16[2,128,256]{2,1,0:T(8,128)(2,1)S(1)}, bf16[2,128,256]{2,1,0:T(8,128)(2,1)S(1)}, u32[]{:S(2)}, u32[]{:S(2)}) %collective-permute-start.1) | collective-permute-done | bytes 131104 | tf_op jit(solution)/shard_map/while/body/eval_jaxpr/ppermute | solution.py:17
  105.6 9.8 %collective-permute-done.2 = bf16[2,512,256]{2,1,0:T(8,128)(2,1)S(1)} collective-permute-done((bf16[2,512,256]{2,1,0:T(8,128)(2,1)S(1)}, bf16[2,512,256]{2,1,0:T(8,128)(2,1)S(1)}, u32[]{:S(2)}, u32[]{:S(2)}) %collective-permute-start.2) | collective-permute-done | bytes 524320 | tf_op jit(solution)/shard_map/while/body/eval_jaxpr/ppermute | solution.py:29
  120.7 2.4 collective-permute-start.1
  124.6 5.6 collective-permute-done.1
  141.3 9.8 %collective-permute-done.2 = bf16[2,512,256]{2,1,0:T(8,128)(2,1)S(1)} collective-permute-done((bf16[2,512,256]{2,1,0:T(8,128)(2,1)S(1)}, bf16[2,512,256]{2,1,0:T(8,128)(2,1)S(1)}, u32[]{:S(2)}, u32[]{:S(2)}) %collective-permute-start.2) | collective-permute-done | bytes 524320 | tf_op jit(solution)/shard_map/while/body/eval_jaxpr/ppermute | solution.py:29
  156.3 2.4 collective-permute-start.1
  160.3 5.6 collective-permute-done.1
  176.9 9.8 %collective-permute-done.2 = bf16[2,512,256]{2,1,0:T(8,128)(2,1)S(1)} collective-permute-done((bf16[2,512,256]{2,1,0:T(8,128)(2,1)S(1)}, bf16[2,512,256]{2,1,0:T(8,128)(2,1)S(1)}, u32[]{:S(2)}, u32[]{:S(2)}) %collective-permute-start.2) | collective-permute-done | bytes 524320 | tf_op jit(solution)/shard_map/while/body/eval_jaxpr/ppermute | solution.py:29
  192.0 2.4 collective-permute-start.1
  195.9 5.6 collective-permute-done.1
  212.6 10.4 %collective-permute-done.2 = bf16[2,512,256]{2,1,0:T(8,128)(2,1)S(1)} collective-permute-done((bf16[2,512,256]{2,1,0:T(8,128)(2,1)S(1)}, bf16[2,512,256]{2,1,0:T(8,128)(2,1)S(1)}, u32[]{:S(2)}, u32[]{:S(2)}) %collective-permute-start.2) | collective-permute-done | bytes 524320 | tf_op jit(solution)/shard_map/while/body/eval_jaxpr/ppermute | solution.py:29
  228.3 2.4 collective-permute-start.1
  232.2 5.6 collective-permute-done.1
  248.9 12.1 %collective-permute-done.2 = bf16[2,512,256]{2,1,0:T(8,128)(2,1)S(1)} collective-permute-done((bf16[2,512,256]{2,1,0:T(8,128)(2,1)S(1)}, bf16[2,512,256]{2,1,0:T(8,128)(2,1)S(1)}, u32[]{:S(2)}, u32[]{:S(2)}) %collective-permute-start.2) | collective-permute-done | bytes 524320 | tf_op jit(solution)/shard_map/while/body/eval_jaxpr/ppermute | solution.py:29
  266.3 2.4 collective-permute-start.1
  270.3 5.6 collective-permute-done.1
  286.9 12.1 %collective-permute-done.2 = bf16[2,512,256]{2,1,0:T(8,128)(2,1)S(1)} collective-permute-done((bf16[2,512,256]{2,1,0:T(8,128)(2,1)S(1)}, bf16[2,512,256]{2,1,0:T(8,128)(2,1)S(1)}, u32[]{:S(2)}, u32[]{:S(2)}) %collective-permute-start.2) | collective-permute-done | bytes 524320 | tf_op jit(solution)/shard_map/while/body/eval_jaxpr/ppermute | solution.py:29
  304.3 2.4 collective-permute-start.1
  308.3 5.6 collective-permute-done.1
  324.9 11.8 %collective-permute-done.2 = bf16[2,512,256]{2,1,0:T(8,128)(2,1)S(1)} collective-permute-done((bf16[2,512,256]{2,1,0:T(8,128)(2,1)S(1)}, bf16[2,512,256]{2,1,0:T(8,128)(2,1)S(1)}, u32[]{:S(2)}, u32[]{:S(2)}) %collective-permute-start.2) | collective-permute-done | bytes 524320 | tf_op jit(solution)/shard_map/while/body/eval_jaxpr/ppermute | solution.py:29
  342.0 2.4 collective-permute-start.1
  346.0 5.6 collective-permute-done.1
  362.6 11.5 %collective-permute-done.2 = bf16[2,512,256]{2,1,0:T(8,128)(2,1)S(1)} collective-permute-done((bf16[2,512,256]{2,1,0:T(8,128)(2,1)S(1)}, bf16[2,512,256]{2,1,0:T(8,128)(2,1)S(1)}, u32[]{:S(2)}, u32[]{:S(2)}) %collective-permute-start.2) | collective-permute-done | bytes 524320 | tf_op jit(solution)/shard_map/while/body/eval_jaxpr/ppermute | solution.py:29
  379.4 2.4 collective-permute-start.1
  383.4 5.6 collective-permute-done.1
  400.0 11.1 %collective-permute-done.2 = bf16[2,512,256]{2,1,0:T(8,128)(2,1)S(1)} collective-permute-done((bf16[2,512,256]{2,1,0:T(8,128)(2,1)S(1)}, bf16[2,512,256]{2,1,0:T(8,128)(2,1)S(1)}, u32[]{:S(2)}, u32[]{:S(2)}) %collective-permute-start.2) | collective-permute-done | bytes 524320 | tf_op jit(solution)/shard_map/while/body/eval_jaxpr/ppermute | solution.py:29
  416.4 2.4 collective-permute-start.1
  420.4 5.6 collective-permute-done.1
  437.1 10.9 %collective-permute-done.2 = bf16[2,512,256]{2,1,0:T(8,128)(2,1)S(1)} collective-permute-done((bf16[2,512,256]{2,1,0:T(8,128)(2,1)S(1)}, bf16[2,512,256]{2,1,0:T(8,128)(2,1)S(1)}, u32[]{:S(2)}, u32[]{:S(2)}) %collective-permute-start.2) | collective-permute-done | bytes 524320 | tf_op jit(solution)/shard_map/while/body/eval_jaxpr/ppermute | solution.py:29
  453.2 2.4 collective-permute-start.1
  457.2 5.6 collective-permute-done.1
  473.8 10.7 %collective-permute-done.2 = bf16[2,512,256]{2,1,0:T(8,128)(2,1)S(1)} collective-permute-done((bf16[2,512,256]{2,1,0:T(8,128)(2,1)S(1)}, bf16[2,512,256]{2,1,0:T(8,128)(2,1)S(1)}, u32[]{:S(2)}, u32[]{:S(2)}) %collective-permute-start.2) | collective-permute-done | bytes 524320 | tf_op jit(solution)/shard_map/while/body/eval_jaxpr/ppermute | solution.py:29
  489.8 2.4 collective-permute-start.1
  493.7 5.6 collective-permute-done.1
  510.4 10.7 %collective-permute-done.2 = bf16[2,512,256]{2,1,0:T(8,128)(2,1)S(1)} collective-permute-done((bf16[2,512,256]{2,1,0:T(8,128)(2,1)S(1)}, bf16[2,512,256]{2,1,0:T(8,128)(2,1)S(1)}, u32[]{:S(2)}, u32[]{:S(2)}) %collective-permute-start.2) | collective-permute-done | bytes 524320 | tf_op jit(solution)/shard_map/while/body/eval_jaxpr/ppermute | solution.py:29
  530.3 5.6 collective-permute-done.1
  547.0 10.8 %collective-permute-done.2 = bf16[2,512,256]{2,1,0:T(8,128)(2,1)S(1)} collective-permute-done((bf16[2,512,256]{2,1,0:T(8,128)(2,1)S(1)}, bf16[2,512,256]{2,1,0:T(8,128)(2,1)S(1)}, u32[]{:S(2)}, u32[]{:S(2)}) %collective-permute-start.2) | collective-permute-done | bytes 524320 | tf_op jit(solution)/shard_map/while/body/eval_jaxpr/ppermute | solution.py:29
  563.1 2.4 collective-permute-start.1
  567.1 5.6 collective-permute-done.1
  583.7 11.0 %collective-permute-done.2 = bf16[2,512,256]{2,1,0:T(8,128)(2,1)S(1)} collective-permute-done((bf16[2,512,256]{2,1,0:T(8,128)(2,1)S(1)}, bf16[2,512,256]{2,1,0:T(8,128)(2,1)S(1)}, u32[]{:S(2)}, u32[]{:S(2)}) %collective-permute-start.2) | collective-permute-done | bytes 524320 | tf_op jit(solution)/shard_map/while/body/eval_jaxpr/ppermute | solution.py:29
  (563 shorter events, 285.3 us)
Async XLA Ops:
  3.5 10.0 %collective-permute-start = (bf16[2,128,256]{2,1,0:T(8,128)(2,1)S(1)}, bf16[2,128,256]{2,1,0:T(8,128)(2,1)S(1)}, u32[]{:S(2)}, u32[]{:S(2)}) collective-permute-start(bf16[2,128,256]{2,1,0:T(8,128)(2,1)S(1)} %select_multiply_fusion.2), channel_id=1, source_target_pairs={{1,0},{2,1},{3,2},{4,3},{5,4},{6,5},{7,6},{8,7},{9,8},{10,9},{11,1... | collective-permute-start | bytes 393224 | tf_op jit(solution)/shard_map/while/body/eval_jaxpr/ppermute | solution.py:19
  10.1 9.6 %collective-permute-start.1 = (bf16[2,128,256]{2,1,0:T(8,128)(2,1)S(1)}, bf16[2,128,256]{2,1,0:T(8,128)(2,1)S(1)}, u32[]{:S(2)}, u32[]{:S(2)}) collective-permute-start(bf16[2,128,256]{2,1,0:T(8,128)(2,1)S(1)} %select_multiply_fusion.2), channel_id=1, source_target_pairs={{0,1},{1,2},{2,3},{3,4},{4,5},{5,6},{6,7},{7,8},{8,9},{9,10},{10,1... | collective-permute-start | bytes 393224 | tf_op jit(solution)/shard_map/while/body/eval_jaxpr/ppermute | solution.py:17
  29.4 11.1 %collective-permute-start.2 = (bf16[2,512,256]{2,1,0:T(8,128)(2,1)S(1)}, bf16[2,512,256]{2,1,0:T(8,128)(2,1)S(1)}, u32[]{:S(2)}, u32[]{:S(2)}) collective-permute-start(bf16[2,512,256]{2,1,0:T(8,128)(2,1)S(1)} %get-tuple-element.420), channel_id=1, source_target_pairs={{0,32},{32,64},{64,96},{96,128},{128,160},{160,192},{192,224},{224... | collective-permute-start | bytes 1572872 | tf_op jit(solution)/shard_map/while/body/eval_jaxpr/ppermute | solution.py:29
  43.8 7.9 %collective-permute-start = (bf16[2,128,256]{2,1,0:T(8,128)(2,1)S(1)}, bf16[2,128,256]{2,1,0:T(8,128)(2,1)S(1)}, u32[]{:S(2)}, u32[]{:S(2)}) collective-permute-start(bf16[2,128,256]{2,1,0:T(8,128)(2,1)S(1)} %select_multiply_fusion.2), channel_id=1, source_target_pairs={{1,0},{2,1},{3,2},{4,3},{5,4},{6,5},{7,6},{8,7},{9,8},{10,9},{11,1... | collective-permute-start | bytes 393224 | tf_op jit(solution)/shard_map/while/body/eval_jaxpr/ppermute | solution.py:19
  48.3 9.6 %collective-permute-start.1 = (bf16[2,128,256]{2,1,0:T(8,128)(2,1)S(1)}, bf16[2,128,256]{2,1,0:T(8,128)(2,1)S(1)}, u32[]{:S(2)}, u32[]{:S(2)}) collective-permute-start(bf16[2,128,256]{2,1,0:T(8,128)(2,1)S(1)} %select_multiply_fusion.2), channel_id=1, source_target_pairs={{0,1},{1,2},{2,3},{3,4},{4,5},{5,6},{6,7},{7,8},{8,9},{9,10},{10,1... | collective-permute-start | bytes 393224 | tf_op jit(solution)/shard_map/while/body/eval_jaxpr/ppermute | solution.py:17
  67.6 11.1 %collective-permute-start.2 = (bf16[2,512,256]{2,1,0:T(8,128)(2,1)S(1)}, bf16[2,512,256]{2,1,0:T(8,128)(2,1)S(1)}, u32[]{:S(2)}, u32[]{:S(2)}) collective-permute-start(bf16[2,512,256]{2,1,0:T(8,128)(2,1)S(1)} %get-tuple-element.420), channel_id=1, source_target_pairs={{0,32},{32,64},{64,96},{96,128},{128,160},{160,192},{192,224},{224... | collective-permute-start | bytes 1572872 | tf_op jit(solution)/shard_map/while/body/eval_jaxpr/ppermute | solution.py:29
  82.0 6.5 %collective-permute-start = (bf16[2,128,256]{2,1,0:T(8,128)(2,1)S(1)}, bf16[2,128,256]{2,1,0:T(8,128)(2,1)S(1)}, u32[]{:S(2)}, u32[]{:S(2)}) collective-permute-start(bf16[2,128,256]{2,1,0:T(8,128)(2,1)S(1)} %select_multiply_fusion.2), channel_id=1, source_target_pairs={{1,0},{2,1},{3,2},{4,3},{5,4},{6,5},{7,6},{8,7},{9,8},{10,9},{11,1... | collective-permute-start | bytes 393224 | tf_op jit(solution)/shard_map/while/body/eval_jaxpr/ppermute | solution.py:19
  85.0 9.6 %collective-permute-start.1 = (bf16[2,128,256]{2,1,0:T(8,128)(2,1)S(1)}, bf16[2,128,256]{2,1,0:T(8,128)(2,1)S(1)}, u32[]{:S(2)}, u32[]{:S(2)}) collective-permute-start(bf16[2,128,256]{2,1,0:T(8,128)(2,1)S(1)} %select_multiply_fusion.2), channel_id=1, source_target_pairs={{0,1},{1,2},{2,3},{3,4},{4,5},{5,6},{6,7},{7,8},{8,9},{9,10},{10,1... | collective-permute-start | bytes 393224 | tf_op jit(solution)/shard_map/while/body/eval_jaxpr/ppermute | solution.py:17
  104.3 11.1 %collective-permute-start.2 = (bf16[2,512,256]{2,1,0:T(8,128)(2,1)S(1)}, bf16[2,512,256]{2,1,0:T(8,128)(2,1)S(1)}, u32[]{:S(2)}, u32[]{:S(2)}) collective-permute-start(bf16[2,512,256]{2,1,0:T(8,128)(2,1)S(1)} %get-tuple-element.420), channel_id=1, source_target_pairs={{0,32},{32,64},{64,96},{96,128},{128,160},{160,192},{192,224},{224... | collective-permute-start | bytes 1572872 | tf_op jit(solution)/shard_map/while/body/eval_jaxpr/ppermute | solution.py:29
  118.7 5.9 collective-permute-start
  120.7 9.6 %collective-permute-start.1 = (bf16[2,128,256]{2,1,0:T(8,128)(2,1)S(1)}, bf16[2,128,256]{2,1,0:T(8,128)(2,1)S(1)}, u32[]{:S(2)}, u32[]{:S(2)}) collective-permute-start(bf16[2,128,256]{2,1,0:T(8,128)(2,1)S(1)} %select_multiply_fusion.2), channel_id=1, source_target_pairs={{0,1},{1,2},{2,3},{3,4},{4,5},{5,6},{6,7},{7,8},{8,9},{9,10},{10,1... | collective-permute-start | bytes 393224 | tf_op jit(solution)/shard_map/while/body/eval_jaxpr/ppermute | solution.py:17
  140.0 11.1 %collective-permute-start.2 = (bf16[2,512,256]{2,1,0:T(8,128)(2,1)S(1)}, bf16[2,512,256]{2,1,0:T(8,128)(2,1)S(1)}, u32[]{:S(2)}, u32[]{:S(2)}) collective-permute-start(bf16[2,512,256]{2,1,0:T(8,128)(2,1)S(1)} %get-tuple-element.420), channel_id=1, source_target_pairs={{0,32},{32,64},{64,96},{96,128},{128,160},{160,192},{192,224},{224... | collective-permute-start | bytes 1572872 | tf_op jit(solution)/shard_map/while/body/eval_jaxpr/ppermute | solution.py:29
  154.4 5.9 collective-permute-start
  156.3 9.6 %collective-permute-start.1 = (bf16[2,128,256]{2,1,0:T(8,128)(2,1)S(1)}, bf16[2,128,256]{2,1,0:T(8,128)(2,1)S(1)}, u32[]{:S(2)}, u32[]{:S(2)}) collective-permute-start(bf16[2,128,256]{2,1,0:T(8,128)(2,1)S(1)} %select_multiply_fusion.2), channel_id=1, source_target_pairs={{0,1},{1,2},{2,3},{3,4},{4,5},{5,6},{6,7},{7,8},{8,9},{9,10},{10,1... | collective-permute-start | bytes 393224 | tf_op jit(solution)/shard_map/while/body/eval_jaxpr/ppermute | solution.py:17
  175.6 11.1 %collective-permute-start.2 = (bf16[2,512,256]{2,1,0:T(8,128)(2,1)S(1)}, bf16[2,512,256]{2,1,0:T(8,128)(2,1)S(1)}, u32[]{:S(2)}, u32[]{:S(2)}) collective-permute-start(bf16[2,512,256]{2,1,0:T(8,128)(2,1)S(1)} %get-tuple-element.420), channel_id=1, source_target_pairs={{0,32},{32,64},{64,96},{96,128},{128,160},{160,192},{192,224},{224... | collective-permute-start | bytes 1572872 | tf_op jit(solution)/shard_map/while/body/eval_jaxpr/ppermute | solution.py:29
  190.1 5.9 collective-permute-start
  192.0 9.6 %collective-permute-start.1 = (bf16[2,128,256]{2,1,0:T(8,128)(2,1)S(1)}, bf16[2,128,256]{2,1,0:T(8,128)(2,1)S(1)}, u32[]{:S(2)}, u32[]{:S(2)}) collective-permute-start(bf16[2,128,256]{2,1,0:T(8,128)(2,1)S(1)} %select_multiply_fusion.2), channel_id=1, source_target_pairs={{0,1},{1,2},{2,3},{3,4},{4,5},{5,6},{6,7},{7,8},{8,9},{9,10},{10,1... | collective-permute-start | bytes 393224 | tf_op jit(solution)/shard_map/while/body/eval_jaxpr/ppermute | solution.py:17
  211.3 11.7 %collective-permute-start.2 = (bf16[2,512,256]{2,1,0:T(8,128)(2,1)S(1)}, bf16[2,512,256]{2,1,0:T(8,128)(2,1)S(1)}, u32[]{:S(2)}, u32[]{:S(2)}) collective-permute-start(bf16[2,512,256]{2,1,0:T(8,128)(2,1)S(1)} %get-tuple-element.420), channel_id=1, source_target_pairs={{0,32},{32,64},{64,96},{96,128},{128,160},{160,192},{192,224},{224... | collective-permute-start | bytes 1572872 | tf_op jit(solution)/shard_map/while/body/eval_jaxpr/ppermute | solution.py:29
  226.3 5.9 collective-permute-start
  228.3 9.6 %collective-permute-start.1 = (bf16[2,128,256]{2,1,0:T(8,128)(2,1)S(1)}, bf16[2,128,256]{2,1,0:T(8,128)(2,1)S(1)}, u32[]{:S(2)}, u32[]{:S(2)}) collective-permute-start(bf16[2,128,256]{2,1,0:T(8,128)(2,1)S(1)} %select_multiply_fusion.2), channel_id=1, source_target_pairs={{0,1},{1,2},{2,3},{3,4},{4,5},{5,6},{6,7},{7,8},{8,9},{9,10},{10,1... | collective-permute-start | bytes 393224 | tf_op jit(solution)/shard_map/while/body/eval_jaxpr/ppermute | solution.py:17
  247.6 13.4 %collective-permute-start.2 = (bf16[2,512,256]{2,1,0:T(8,128)(2,1)S(1)}, bf16[2,512,256]{2,1,0:T(8,128)(2,1)S(1)}, u32[]{:S(2)}, u32[]{:S(2)}) collective-permute-start(bf16[2,512,256]{2,1,0:T(8,128)(2,1)S(1)} %get-tuple-element.420), channel_id=1, source_target_pairs={{0,32},{32,64},{64,96},{96,128},{128,160},{160,192},{192,224},{224... | collective-permute-start | bytes 1572872 | tf_op jit(solution)/shard_map/while/body/eval_jaxpr/ppermute | solution.py:29
  264.4 5.9 collective-permute-start
  266.3 9.6 %collective-permute-start.1 = (bf16[2,128,256]{2,1,0:T(8,128)(2,1)S(1)}, bf16[2,128,256]{2,1,0:T(8,128)(2,1)S(1)}, u32[]{:S(2)}, u32[]{:S(2)}) collective-permute-start(bf16[2,128,256]{2,1,0:T(8,128)(2,1)S(1)} %select_multiply_fusion.2), channel_id=1, source_target_pairs={{0,1},{1,2},{2,3},{3,4},{4,5},{5,6},{6,7},{7,8},{8,9},{9,10},{10,1... | collective-permute-start | bytes 393224 | tf_op jit(solution)/shard_map/while/body/eval_jaxpr/ppermute | solution.py:17
  285.6 13.4 %collective-permute-start.2 = (bf16[2,512,256]{2,1,0:T(8,128)(2,1)S(1)}, bf16[2,512,256]{2,1,0:T(8,128)(2,1)S(1)}, u32[]{:S(2)}, u32[]{:S(2)}) collective-permute-start(bf16[2,512,256]{2,1,0:T(8,128)(2,1)S(1)} %get-tuple-element.420), channel_id=1, source_target_pairs={{0,32},{32,64},{64,96},{96,128},{128,160},{160,192},{192,224},{224... | collective-permute-start | bytes 1572872 | tf_op jit(solution)/shard_map/while/body/eval_jaxpr/ppermute | solution.py:29
  302.4 5.9 collective-permute-start
  304.3 9.6 %collective-permute-start.1 = (bf16[2,128,256]{2,1,0:T(8,128)(2,1)S(1)}, bf16[2,128,256]{2,1,0:T(8,128)(2,1)S(1)}, u32[]{:S(2)}, u32[]{:S(2)}) collective-permute-start(bf16[2,128,256]{2,1,0:T(8,128)(2,1)S(1)} %select_multiply_fusion.2), channel_id=1, source_target_pairs={{0,1},{1,2},{2,3},{3,4},{4,5},{5,6},{6,7},{7,8},{8,9},{9,10},{10,1... | collective-permute-start | bytes 393224 | tf_op jit(solution)/shard_map/while/body/eval_jaxpr/ppermute | solution.py:17
  323.6 13.1 %collective-permute-start.2 = (bf16[2,512,256]{2,1,0:T(8,128)(2,1)S(1)}, bf16[2,512,256]{2,1,0:T(8,128)(2,1)S(1)}, u32[]{:S(2)}, u32[]{:S(2)}) collective-permute-start(bf16[2,512,256]{2,1,0:T(8,128)(2,1)S(1)} %get-tuple-element.420), channel_id=1, source_target_pairs={{0,32},{32,64},{64,96},{96,128},{128,160},{160,192},{192,224},{224... | collective-permute-start | bytes 1572872 | tf_op jit(solution)/shard_map/while/body/eval_jaxpr/ppermute | solution.py:29
  340.1 5.9 collective-permute-start
  342.0 9.6 %collective-permute-start.1 = (bf16[2,128,256]{2,1,0:T(8,128)(2,1)S(1)}, bf16[2,128,256]{2,1,0:T(8,128)(2,1)S(1)}, u32[]{:S(2)}, u32[]{:S(2)}) collective-permute-start(bf16[2,128,256]{2,1,0:T(8,128)(2,1)S(1)} %select_multiply_fusion.2), channel_id=1, source_target_pairs={{0,1},{1,2},{2,3},{3,4},{4,5},{5,6},{6,7},{7,8},{8,9},{9,10},{10,1... | collective-permute-start | bytes 393224 | tf_op jit(solution)/shard_map/while/body/eval_jaxpr/ppermute | solution.py:17
  361.3 12.8 %collective-permute-start.2 = (bf16[2,512,256]{2,1,0:T(8,128)(2,1)S(1)}, bf16[2,512,256]{2,1,0:T(8,128)(2,1)S(1)}, u32[]{:S(2)}, u32[]{:S(2)}) collective-permute-start(bf16[2,512,256]{2,1,0:T(8,128)(2,1)S(1)} %get-tuple-element.420), channel_id=1, source_target_pairs={{0,32},{32,64},{64,96},{96,128},{128,160},{160,192},{192,224},{224... | collective-permute-start | bytes 1572872 | tf_op jit(solution)/shard_map/while/body/eval_jaxpr/ppermute | solution.py:29
  377.5 5.9 collective-permute-start
  379.4 9.6 %collective-permute-start.1 = (bf16[2,128,256]{2,1,0:T(8,128)(2,1)S(1)}, bf16[2,128,256]{2,1,0:T(8,128)(2,1)S(1)}, u32[]{:S(2)}, u32[]{:S(2)}) collective-permute-start(bf16[2,128,256]{2,1,0:T(8,128)(2,1)S(1)} %select_multiply_fusion.2), channel_id=1, source_target_pairs={{0,1},{1,2},{2,3},{3,4},{4,5},{5,6},{6,7},{7,8},{8,9},{9,10},{10,1... | collective-permute-start | bytes 393224 | tf_op jit(solution)/shard_map/while/body/eval_jaxpr/ppermute | solution.py:17
  398.7 12.5 %collective-permute-start.2 = (bf16[2,512,256]{2,1,0:T(8,128)(2,1)S(1)}, bf16[2,512,256]{2,1,0:T(8,128)(2,1)S(1)}, u32[]{:S(2)}, u32[]{:S(2)}) collective-permute-start(bf16[2,512,256]{2,1,0:T(8,128)(2,1)S(1)} %get-tuple-element.420), channel_id=1, source_target_pairs={{0,32},{32,64},{64,96},{96,128},{128,160},{160,192},{192,224},{224... | collective-permute-start | bytes 1572872 | tf_op jit(solution)/shard_map/while/body/eval_jaxpr/ppermute | solution.py:29
  414.5 5.9 collective-permute-start
  416.4 9.6 %collective-permute-start.1 = (bf16[2,128,256]{2,1,0:T(8,128)(2,1)S(1)}, bf16[2,128,256]{2,1,0:T(8,128)(2,1)S(1)}, u32[]{:S(2)}, u32[]{:S(2)}) collective-permute-start(bf16[2,128,256]{2,1,0:T(8,128)(2,1)S(1)} %select_multiply_fusion.2), channel_id=1, source_target_pairs={{0,1},{1,2},{2,3},{3,4},{4,5},{5,6},{6,7},{7,8},{8,9},{9,10},{10,1... | collective-permute-start | bytes 393224 | tf_op jit(solution)/shard_map/while/body/eval_jaxpr/ppermute | solution.py:17
  435.8 12.2 %collective-permute-start.2 = (bf16[2,512,256]{2,1,0:T(8,128)(2,1)S(1)}, bf16[2,512,256]{2,1,0:T(8,128)(2,1)S(1)}, u32[]{:S(2)}, u32[]{:S(2)}) collective-permute-start(bf16[2,512,256]{2,1,0:T(8,128)(2,1)S(1)} %get-tuple-element.420), channel_id=1, source_target_pairs={{0,32},{32,64},{64,96},{96,128},{128,160},{160,192},{192,224},{224... | collective-permute-start | bytes 1572872 | tf_op jit(solution)/shard_map/while/body/eval_jaxpr/ppermute | solution.py:29
  451.3 5.9 collective-permute-start
  453.2 9.6 %collective-permute-start.1 = (bf16[2,128,256]{2,1,0:T(8,128)(2,1)S(1)}, bf16[2,128,256]{2,1,0:T(8,128)(2,1)S(1)}, u32[]{:S(2)}, u32[]{:S(2)}) collective-permute-start(bf16[2,128,256]{2,1,0:T(8,128)(2,1)S(1)} %select_multiply_fusion.2), channel_id=1, source_target_pairs={{0,1},{1,2},{2,3},{3,4},{4,5},{5,6},{6,7},{7,8},{8,9},{9,10},{10,1... | collective-permute-start | bytes 393224 | tf_op jit(solution)/shard_map/while/body/eval_jaxpr/ppermute | solution.py:17
  472.5 12.0 %collective-permute-start.2 = (bf16[2,512,256]{2,1,0:T(8,128)(2,1)S(1)}, bf16[2,512,256]{2,1,0:T(8,128)(2,1)S(1)}, u32[]{:S(2)}, u32[]{:S(2)}) collective-permute-start(bf16[2,512,256]{2,1,0:T(8,128)(2,1)S(1)} %get-tuple-element.420), channel_id=1, source_target_pairs={{0,32},{32,64},{64,96},{96,128},{128,160},{160,192},{192,224},{224... | collective-permute-start | bytes 1572872 | tf_op jit(solution)/shard_map/while/body/eval_jaxpr/ppermute | solution.py:29
  487.9 5.9 collective-permute-start
  489.8 9.6 %collective-permute-start.1 = (bf16[2,128,256]{2,1,0:T(8,128)(2,1)S(1)}, bf16[2,128,256]{2,1,0:T(8,128)(2,1)S(1)}, u32[]{:S(2)}, u32[]{:S(2)}) collective-permute-start(bf16[2,128,256]{2,1,0:T(8,128)(2,1)S(1)} %select_multiply_fusion.2), channel_id=1, source_target_pairs={{0,1},{1,2},{2,3},{3,4},{4,5},{5,6},{6,7},{7,8},{8,9},{9,10},{10,1... | collective-permute-start | bytes 393224 | tf_op jit(solution)/shard_map/while/body/eval_jaxpr/ppermute | solution.py:17
  509.1 12.0 %collective-permute-start.2 = (bf16[2,512,256]{2,1,0:T(8,128)(2,1)S(1)}, bf16[2,512,256]{2,1,0:T(8,128)(2,1)S(1)}, u32[]{:S(2)}, u32[]{:S(2)}) collective-permute-start(bf16[2,512,256]{2,1,0:T(8,128)(2,1)S(1)} %get-tuple-element.420), channel_id=1, source_target_pairs={{0,32},{32,64},{64,96},{96,128},{128,160},{160,192},{192,224},{224... | collective-permute-start | bytes 1572872 | tf_op jit(solution)/shard_map/while/body/eval_jaxpr/ppermute | solution.py:29
  524.4 5.9 collective-permute-start
  526.4 9.6 %collective-permute-start.1 = (bf16[2,128,256]{2,1,0:T(8,128)(2,1)S(1)}, bf16[2,128,256]{2,1,0:T(8,128)(2,1)S(1)}, u32[]{:S(2)}, u32[]{:S(2)}) collective-permute-start(bf16[2,128,256]{2,1,0:T(8,128)(2,1)S(1)} %select_multiply_fusion.2), channel_id=1, source_target_pairs={{0,1},{1,2},{2,3},{3,4},{4,5},{5,6},{6,7},{7,8},{8,9},{9,10},{10,1... | collective-permute-start | bytes 393224 | tf_op jit(solution)/shard_map/while/body/eval_jaxpr/ppermute | solution.py:17
  545.7 12.1 %collective-permute-start.2 = (bf16[2,512,256]{2,1,0:T(8,128)(2,1)S(1)}, bf16[2,512,256]{2,1,0:T(8,128)(2,1)S(1)}, u32[]{:S(2)}, u32[]{:S(2)}) collective-permute-start(bf16[2,512,256]{2,1,0:T(8,128)(2,1)S(1)} %get-tuple-element.420), channel_id=1, source_target_pairs={{0,32},{32,64},{64,96},{96,128},{128,160},{160,192},{192,224},{224... | collective-permute-start | bytes 1572872 | tf_op jit(solution)/shard_map/while/body/eval_jaxpr/ppermute | solution.py:29
  561.2 5.9 collective-permute-start
  563.1 9.6 %collective-permute-start.1 = (bf16[2,128,256]{2,1,0:T(8,128)(2,1)S(1)}, bf16[2,128,256]{2,1,0:T(8,128)(2,1)S(1)}, u32[]{:S(2)}, u32[]{:S(2)}) collective-permute-start(bf16[2,128,256]{2,1,0:T(8,128)(2,1)S(1)} %select_multiply_fusion.2), channel_id=1, source_target_pairs={{0,1},{1,2},{2,3},{3,4},{4,5},{5,6},{6,7},{7,8},{8,9},{9,10},{10,1... | collective-permute-start | bytes 393224 | tf_op jit(solution)/shard_map/while/body/eval_jaxpr/ppermute | solution.py:17
  582.4 12.3 %collective-permute-start.2 = (bf16[2,512,256]{2,1,0:T(8,128)(2,1)S(1)}, bf16[2,512,256]{2,1,0:T(8,128)(2,1)S(1)}, u32[]{:S(2)}, u32[]{:S(2)}) collective-permute-start(bf16[2,512,256]{2,1,0:T(8,128)(2,1)S(1)} %get-tuple-element.420), channel_id=1, source_target_pairs={{0,32},{32,64},{64,96},{96,128},{128,160},{160,192},{192,224},{224... | collective-permute-start | bytes 1572872 | tf_op jit(solution)/shard_map/while/body/eval_jaxpr/ppermute | solution.py:29
  (96 other events, 458.2 us)
where the time goes:
time: 605 us; the launch traced here: 595 us
  waiting for transfers between devices  264 us (44%)
  local copies, waits for them, and re-layouts  110 us (18%)
  starting transfers between devices  96.7 us (16%)
  other arithmetic  78.8 us (13%)
  matrix products  43.1 us (7%)
    ppermute x16, waiting for transfers between devices, from_behind(): return lax.ppermute(x, axis, pairs)  172 us
    ppermute x16, waiting for transfers between devices, extended_2(): lax.ppermute(tail, axis, [(i, (i + 1) % count) for i in range(count)])  91.8 us
    ppermute x16, starting transfers between devices, extended_2(): lax.ppermute(head, axis, [((i + 1) % count, i) for i in range(count)])  39 us
    gather x48, local copies, waits for them, and re-layouts, gcn_layer(): picked = jnp.take_along_axis(source_pool, sources[:, :, None, None], axis=1)  37.7 us
    ppermute x16, starting transfers between devices, extended_2(): lax.ppermute(tail, axis, [(i, (i + 1) % count) for i in range(count)])  37 us
    dot_general x16, matrix products, gcn_layer(): jnp.einsum('cntk,cnkd->cntd', adjacency, picked, preferred_element_type=j...  35.5 us
    convert_element_type x16, other arithmetic, finish_rows(): blended.astype(jnp.bfloat16).reshape(count_spans * row_count, width)  27.4 us
    gather x16, local copies, waits for them, and re-layouts, build_pool(): jnp.take_along_axis(hidden, boundary_rows[:, :, None], axis=1)  26.5 us
  transfers between devices with their start and end apart: 48, of which 32 were waited for; matrix products, arithmetic and copies ran while one was open for 4% of the time, Pallas kernels for 0%

commit v1 on v0

v1 whole, which is shorter than its diff:
```python
import jax
import jax.numpy as jnp
import numpy as np
from jax import lax
from jax.experimental import pallas as pl
from jax.experimental.pallas import tpu as pltpu
from jax.sharding import PartitionSpec as P

MESH = pl.DeviceIdType.MESH

alpha_mix = 0.1
lambda_decay = 0.5

SPANS = 2
ROWS = 512
TILE = 128
WIDTH = 256
RIM = 128
OWN = ROWS // TILE
POOL = ROWS + 2 * RIM
CHUNK = 256


def dot(a, b):
    return jnp.dot(a, b, preferred_element_type=jnp.float32)


def layers_kernel(
    sections,
    shards,
    betas_ref,
    sources_ref,
    count_ref,
    rows_ref,
    initial_ref,
    adjacency_ref,
    weight_ref,
    out_ref,
    weights,
    pool,
    rims,
    full_adj,
    rim_adj,
    rim_send,
    rim_recv,
    down_send,
    down_recv,
    up_send,
    up_recv,
    side_send,
    side_recv,
    out_sem,
):
    z = lax.axis_index("section")
    p = lax.axis_index("node")
    core = lax.rem(p, 2)
    sibling = p + 1 - 2 * core
    before, after = lax.rem(p + shards - 1, shards), lax.rem(p + 1, shards)
    below, above = lax.rem(z + sections - 1, sections), lax.rem(z + 1, sections)
    down_steps = sections // 2
    up_steps = sections - 1 - down_steps

    barrier = pltpu.get_barrier_semaphore()
    for neighbour in ((z, before), (z, after), (below, p), (above, p)):
        pl.semaphore_signal(barrier, inc=1, device_id=neighbour, device_id_type=MESH)

    def down_copy(step):
        index = lax.rem(z + step - 1, sections)
        return pltpu.make_async_remote_copy(
            src_ref=weights.at[index, core],
            dst_ref=weights.at[index, core],
            send_sem=down_send.at[step - 1],
            recv_sem=down_recv.at[step - 1],
            device_id=(below, p),
            device_id_type=MESH,
        )

    def down_arrival(step):
        index = lax.rem(z + step, sections)
        return pltpu.make_async_remote_copy(
            src_ref=weights.at[index, core],
            dst_ref=weights.at[index, core],
            send_sem=down_send.at[step - 1],
            recv_sem=down_recv.at[step - 1],
            device_id=(below, p),
            device_id_type=MESH,
        )

    def up_copy(step):
        index = lax.rem(z - step + 1 + sections, sections)
        return pltpu.make_async_remote_copy(
            src_ref=weights.at[index, core],
            dst_ref=weights.at[index, core],
            send_sem=up_send.at[step - 1],
            recv_sem=up_recv.at[step - 1],
            device_id=(above, p),
            device_id_type=MESH,
        )

    def up_arrival(step):
        index = lax.rem(z - step + sections, sections)
        return pltpu.make_async_remote_copy(
            src_ref=weights.at[index, core],
            dst_ref=weights.at[index, core],
            send_sem=up_send.at[step - 1],
            recv_sem=up_recv.at[step - 1],
            device_id=(above, p),
            device_id_type=MESH,
        )

    def side_copy(index):
        return pltpu.make_async_remote_copy(
            src_ref=weights.at[index, core],
            dst_ref=weights.at[index, core],
            send_sem=side_send.at[index],
            recv_sem=side_recv.at[index],
            device_id=(z, sibling),
            device_id_type=MESH,
        )

    def side_arrival(index):
        return pltpu.make_async_remote_copy(
            src_ref=weights.at[index, core],
            dst_ref=weights.at[index, 1 - core],
            send_sem=side_send.at[index],
            recv_sem=side_recv.at[index],
            device_id=(z, sibling),
            device_id_type=MESH,
        )

    def relay(step):
        down_arrival(step).wait_recv()

        @pl.when(step < down_steps)
        def _():
            down_copy(step + 1).start()

        @pl.when(z + step >= sections)
        def _():
            side_copy(z + step - sections).start()

        @pl.when(step <= up_steps)
        def _():
            up_arrival(step).wait_recv()

            @pl.when(step < up_steps)
            def _():
                up_copy(step + 1).start()

            @pl.when(z - step >= 0)
            def _():
                side_copy(z - step).start()

    def rim_copies(layer, span):
        to_after = pltpu.make_async_remote_copy(
            src_ref=rims.at[layer, span],
            dst_ref=pool.at[layer, span, pl.ds(ROWS, RIM)],
            send_sem=rim_send.at[layer, span, 0],
            recv_sem=rim_recv.at[layer, span, 0],
            device_id=(z, after),
            device_id_type=MESH,
        )
        to_before = pltpu.make_async_remote_copy(
            src_ref=rims.at[layer, span],
            dst_ref=pool.at[layer, span, pl.ds(ROWS + RIM, RIM)],
            send_sem=rim_send.at[layer, span, 1],
            recv_sem=rim_recv.at[layer, span, 1],
            device_id=(z, before),
            device_id_type=MESH,
        )
        return to_after, to_before

    weights[z] = weight_ref[0].reshape(2, WIDTH // 2, WIDTH)

    lane = lax.broadcasted_iota(jnp.int32, (RIM, TILE), 1)
    row = lax.broadcasted_iota(jnp.int32, (RIM, TILE), 0)
    picks = []
    for span in range(SPANS):
        wanted = jnp.broadcast_to(rows_ref[span : span + 1, :], (RIM, RIM)).T
        wanted = jnp.where(row < count_ref[span, 0], wanted, -1)
        pick = jnp.concatenate(
            [jnp.where(wanted == lane + t * TILE, 1.0, 0.0) for t in range(OWN)], axis=1
        ).astype(jnp.bfloat16)
        picks.append(pick)
        rims[0, span] = dot(pick, initial_ref[span]).astype(jnp.bfloat16)

    pl.semaphore_wait(barrier, 4)
    for span in range(SPANS):
        for copy in rim_copies(0, span):
            copy.start()
    down_copy(1).start()
    up_copy(1).start()

    for span in range(SPANS):
        pool[0, span, pl.ds(0, ROWS)] = initial_ref[span]
        for block in range(OWN):
            first = sources_ref[span, 3 * block]
            second = sources_ref[span, 3 * block + 1]
            third = sources_ref[span, 3 * block + 2]
            at_before = jnp.where(second == OWN, 1, 0) + jnp.where(third == OWN, 2, 0)
            at_after = jnp.where(second == OWN + 1, 1, 0) + jnp.where(third == OWN + 1, 2, 0)
            at_own = jnp.minimum(3 - at_before - at_after, 2)
            own_tile = first + second + third - (2 * OWN + 1)
            place = pl.ds(block * TILE, TILE)
            own = adjacency_ref[span, 3 * block + at_own]
            for t in range(OWN):
                full_adj[span, place, t * TILE : (t + 1) * TILE] = jnp.where(
                    own_tile == t, own, jnp.zeros_like(own)
                )
            full_adj[span, place, ROWS : ROWS + RIM] = adjacency_ref[span, 3 * block + at_before]
            full_adj[span, place, ROWS + RIM : POOL] = adjacency_ref[span, 3 * block + at_after]
        rim_adj[span] = dot(picks[span], full_adj[span]).astype(jnp.bfloat16)

    def finish(aggregate, anchor, weight, mixing):
        blended = (1.0 - alpha_mix) * aggregate + alpha_mix * anchor.astype(jnp.float32)
        projected = dot(blended.astype(jnp.bfloat16), weight)
        return jnp.maximum((1.0 - mixing) * blended + mixing * projected, 0.0).astype(jnp.bfloat16)

    def all_rows(layer, span, mixing):
        weight = weights[layer].reshape(WIDTH, WIDTH)
        for start in range(0, ROWS, CHUNK):
            place = pl.ds(start, CHUNK)
            aggregate = dot(full_adj[span, place, :], pool[layer, span])
            pool[layer + 1, span, place] = finish(
                aggregate, initial_ref[span, place], weight, mixing
            )

    first_steps = jnp.minimum(sections - z, down_steps)
    lax.fori_loop(1, first_steps + 1, lambda step, c: (relay(step), c)[1], 0)

    def layer_step(layer, carry):
        mixing = betas_ref[layer]
        step = sections - z + layer

        @pl.when((layer >= 1) & (step <= down_steps))
        def _():
            relay(step)

        @pl.when(layer < z)
        def _():
            side_arrival(layer).wait_recv()

        for span in range(SPANS):
            own_part = dot(rim_adj[span, :, 0:ROWS], pool[layer, span, pl.ds(0, ROWS)])
            for copy in rim_copies(layer, span):
                copy.wait_recv()

            @pl.when(layer < z)
            def _():
                aggregate = own_part + dot(
                    rim_adj[span, :, ROWS:POOL], pool[layer, span, pl.ds(ROWS, 2 * RIM)]
                )
                weight = weights[layer].reshape(WIDTH, WIDTH)
                rims[layer + 1, span] = finish(aggregate, rims[0, span], weight, mixing)
                for copy in rim_copies(layer + 1, span):
                    copy.start()

        for span in range(SPANS):
            all_rows(layer, span, mixing)
            for copy in rim_copies(layer, span):
                copy.wait_send()
        return carry

    lax.fori_loop(0, z + 1, layer_step, 0)

    outs = [
        pltpu.make_async_copy(
            pool.at[z + 1, span, pl.ds(0, ROWS)], out_ref.at[0, span], out_sem.at[span]
        )
        for span in range(SPANS)
    ]
    for copy in outs:
        copy.start()

    lax.fori_loop(1, down_steps + 1, lambda step, c: (down_copy(step).wait_send(), c)[1], 0)
    lax.fori_loop(1, up_steps + 1, lambda step, c: (up_copy(step).wait_send(), c)[1], 0)
    lax.fori_loop(0, z, lambda index, c: (side_copy(index).wait_send(), c)[1], 0)
    for copy in outs:
        copy.wait()


def solution(mesh):
    sections, shards = mesh.shape["section"], mesh.shape["node"]
    ordinals = np.arange(sections, dtype=np.float32)
    betas = np.log(np.float32(lambda_decay) / (ordinals + np.float32(1.0)) + np.float32(1.0))

    def on_device(initial, adjacency, sources, boundary_rows, boundary_count, layer_weights):
        def body(*refs):
            layers_kernel(sections, shards, *refs)

        down_steps = sections // 2
        smem = pl.BlockSpec(memory_space=pltpu.SMEM)
        vmem = pl.BlockSpec(memory_space=pltpu.VMEM)
        dma = pltpu.SemaphoreType.DMA
        return pl.pallas_call(
            body,
            out_shape=jax.ShapeDtypeStruct((1, SPANS, ROWS, WIDTH), jnp.bfloat16),
            in_specs=[smem, smem, smem, vmem, vmem, vmem, vmem],
            out_specs=pl.BlockSpec(memory_space=pl.ANY),
            scratch_shapes=[
                pltpu.VMEM((sections, 2, WIDTH // 2, WIDTH), jnp.bfloat16),
                pltpu.VMEM((sections + 1, SPANS, POOL, WIDTH), jnp.bfloat16),
                pltpu.VMEM((sections, SPANS, RIM, WIDTH), jnp.bfloat16),
                pltpu.VMEM((SPANS, ROWS, POOL), jnp.bfloat16),
                pltpu.VMEM((SPANS, RIM, POOL), jnp.bfloat16),
                dma((sections, SPANS, 2)),
                dma((sections, SPANS, 2)),
                dma((down_steps,)),
                dma((down_steps,)),
                dma((down_steps,)),
                dma((down_steps,)),
                dma((sections,)),
                dma((sections,)),
                dma((SPANS,)),
            ],
            compiler_params=pltpu.CompilerParams(
                collective_id=0, has_side_effects=True, vmem_limit_bytes=48 * 1024 * 1024
            ),
        )(
            jnp.asarray(betas, jnp.float32),
            sources,
            boundary_count,
            boundary_rows,
            initial,
            adjacency,
            layer_weights,
        )

    in_specs = (
        P(None, "node", None),
        P(None, "node", None, None),
        P(None, "node"),
        P(None, "node"),
        P(None, "node"),
        P("section", None, None),
    )
    out_specs = P("section", None, "node", None)
    return jax.shard_map(
        on_device, mesh=mesh, in_specs=in_specs, out_specs=out_specs, check_vma=False
    )
```

time: 605 us -> 93 us (0.15); the launches traced: 595 us -> 92.8 us
  waiting for transfers between devices: 264 us -> 0 us
  local copies, waits for them, and re-layouts: 110 us -> 5.33 us
  starting transfers between devices: 96.7 us -> 0 us
  Pallas kernels: 0 us -> 87.5 us
  other arithmetic: 78.8 us -> 0 us
  matrix products: 43.1 us -> 0 us
    ppermute x48 -> x0, waiting for transfers between devices: 264 us -> none  [the longest x16 172 us: from_behind(): return lax.ppermute(x, axis, pairs)]
    ppermute x48 -> x0, starting transfers between devices: 96.7 us -> none  [the longest x16 39 us: extended_2(): lax.ppermute(head, axis, [((i + 1) % count, i) for i in range(count)])]
    pallas_call x0 -> x1, Pallas kernels: none -> 87.5 us  [on_device(): pl.pallas_call(body, out_shape=jax.ShapeDtypeStruct((1, SPANS, ROWS, WIDT...]
    gather x64 -> x0, local copies, waits for them, and re-layouts: 64.3 us -> none  [the longest x48 37.7 us: gcn_layer(): picked = jnp.take_along_axis(source_pool, sources[:, :, None, None], axis=1)]
    dot_general x32 -> x0, matrix products: 43.1 us -> none  [the longest x16 35.5 us: gcn_layer(): jnp.einsum('cntk,cnkd->cntd', adjacency, picked, preferred_element_type=j...]
    convert_element_type x32 -> x0, other arithmetic: 39.7 us -> none  [the longest x16 27.4 us: finish_rows(): blended.astype(jnp.bfloat16).reshape(count_spans * row_count, width)]
    mul x32 -> x0, local copies, waits for them, and re-layouts: 26.3 us -> none  [the longest x16 21 us: finish_rows(): alpha_mix * anchor.astype(jnp.float32)]
    reduce_sum x16 -> x0, other arithmetic: 20 us -> none  [gcn_layer(): aggregate = products.reshape(count_spans, row_count // tile_size, per_row...]
  transfers between devices with their start and end apart: 48 -> 0, of which waited for: 32 -> 0; matrix products, arithmetic and copies ran while one was open for 4% -> 0% of each run, Pallas kernels for 0% -> 0%
where the time goes in v1:
time: 93 us; the launch traced here: 92.8 us
  Pallas kernels  87.5 us (94%)
  local copies, waits for them, and re-layouts  5.33 us (6%)
    pallas_call x1, Pallas kernels, on_device(): pl.pallas_call(body, out_shape=jax.ShapeDtypeStruct((1, SPANS, ROWS, WIDT...  87.5 us
    unnamed x14, local copies, waits for them, and re-layouts  5.33 us

profile of v1, /device:TPU:480, one launch (start us, length us, event | category | flops | bytes accessed | tf_op | source)
XLA Modules:
  0.0 92.8 jit_solution(17685436606735222224)
XLA Ops:
  0.0 0.0 copy-start.5
  0.0 0.0 copy-start.3
  0.0 0.8 copy.8.refs_2_
  0.8 0.0 copy-done.5
  0.8 0.0 copy-done.3
  0.8 0.0 copy-start
  0.8 1.1 %copy-done = bf16[2,12,128,128]{3,2,1,0:T(8,128)(2,1)S(1)} copy-done((bf16[2,12,128,128]{3,2,1,0:T(8,128)(2,1)S(1)}, bf16[2,12,128,128]{3,2,1,0:T(8,128)(2,1)}, u32[]{:S(2)}) %copy-start) | copy-done | bytes 786456
  1.9 0.0 copy-start.1
  1.9 1.0 %copy-done.1 = bf16[2,512,256]{2,1,0:T(8,128)(2,1)S(1)} copy-done((bf16[2,512,256]{2,1,0:T(8,128)(2,1)S(1)}, bf16[2,512,256]{2,1,0:T(8,128)(2,1)}, u32[]{:S(2)}) %copy-start.1) | copy-done | bytes 524312
  3.0 0.0 copy-start.2
  3.0 0.9 copy-done.2
  3.9 0.0 copy-start.4
  3.9 0.7 copy-done.4
  4.5 87.5 %shard_map.73 = bf16[1,2,512,256]{3,2,1,0:T(8,128)(2,1)S(1)} custom-call(f32[16]{0:T(128)S(1)} %copy-done.5, s32[2,12]{1,0:T(2,128)S(1)} %copy-done.3, s32[2,1]{1,0:T(2,128)S(1)} %copy.8.refs_2_, s32[2,128]{1,0:T(2,128)S(1)} %copy-done.4, bf16[2,512,256]{2,1,0:T(8,128)(2,1)S(1)} %copy-done.1, bf16[2,12,128,128]{3,2,1,0:T(8,128)(2,1)S(1)} %copy-done, ...), custom_call_target="tpu_custom_call" | custom-call | tf_op jit(solution)/shard_map/pallas_call | solution.py:295
  92.0 0.8 copy.10
Async XLA Ops:
  0.0 0.8 copy-start.5
  0.0 0.8 copy-start.3
  0.8 1.1 %copy-start = (bf16[2,12,128,128]{3,2,1,0:T(8,128)(2,1)S(1)}, bf16[2,12,128,128]{3,2,1,0:T(8,128)(2,1)}, u32[]{:S(2)}) copy-start(bf16[2,12,128,128]{3,2,1,0:T(8,128)(2,1)} %refs_5_.1) | copy-start | bytes 2359300
  1.9 1.0 %copy-start.1 = (bf16[2,512,256]{2,1,0:T(8,128)(2,1)S(1)}, bf16[2,512,256]{2,1,0:T(8,128)(2,1)}, u32[]{:S(2)}) copy-start(bf16[2,512,256]{2,1,0:T(8,128)(2,1)} %refs_4_.1) | copy-start | bytes 1572868
  3.0 0.9 copy-start.2
  3.9 0.7 copy-start.4

commit v2 on v0

v2 whole, which is shorter than its diff:
```python
import jax
import jax.numpy as jnp
import numpy as np
from jax import lax
from jax.experimental import pallas as pl
from jax.experimental.pallas import tpu as pltpu
from jax.sharding import PartitionSpec as P

MESH = pl.DeviceIdType.MESH

alpha_mix = 0.1
lambda_decay = 0.5

SPANS = 2
ROWS = 512
TILE = 128
WIDTH = 256
RIM = 128
OWN = ROWS // TILE
POOL = ROWS + 2 * RIM
PIECES = 4
PIECE = WIDTH // PIECES
NOTES = 24
AHEAD = 3

ALL = pl.ds(0, ROWS)
FAR = pl.ds(ROWS, RIM)
NEAR = pl.ds(ROWS + RIM, RIM)
EDGES = pl.ds(ROWS, 2 * RIM)


def dot(a, b):
    return jnp.dot(a, b, preferred_element_type=jnp.float32)


def layers_kernel(
    sections,
    shards,
    row_shards,
    betas_ref,
    sources_ref,
    count_ref,
    rows_ref,
    initial_ref,
    adjacency_ref,
    weight_ref,
    out_ref,
    weights,
    pool,
    wide,
    edge,
    tight,
    notes,
    rim_wide,
    rim_edge,
    early,
    ship_send,
    ship_recv,
    rim_send,
    rim_recv,
    direct_send,
    direct_recv,
    share_send,
    share_recv,
    out_send,
    out_recv,
):
    z = lax.axis_index("section")
    p = lax.axis_index("node")
    span = lax.rem(z, 2)
    core = lax.rem(p, 2)
    shadow = lax.rem(p - 1 + 2 * core + shards, shards)
    sibling = p + 1 - 2 * core
    far_to = lax.rem(p + 2 - 4 * core + shards, shards)
    far_from = lax.rem(p - 2 + 4 * core + shards, shards)
    half = lax.rem(p // row_shards, 2)
    beside = p + row_shards - 2 * row_shards * half
    beside_sibling = beside + 1 - 2 * core
    piece = 2 * half + core
    others = (
        (sibling, 2 * half + 1 - core),
        (beside, 2 * (1 - half) + core),
        (beside_sibling, 2 * (1 - half) + 1 - core),
    )
    pair = z + 1 - 2 * span
    layers = z + 2 - span

    barrier = pltpu.get_barrier_semaphore()
    for node in (sibling, far_to, far_from, shadow, beside, beside_sibling):
        pl.semaphore_signal(barrier, inc=1, device_id=(z, node), device_id_type=MESH)

    def greet(step, carry):
        there = lax.rem(z + step, sections)
        pl.semaphore_signal(barrier, inc=1, device_id=(there, p), device_id_type=MESH)
        return carry

    lax.fori_loop(1, sections, greet, 0)

    def remote(src, dst, send, recv, device):
        return pltpu.make_async_remote_copy(
            src_ref=src,
            dst_ref=dst,
            send_sem=send,
            recv_sem=recv,
            device_id=device,
            device_id_type=MESH,
        )

    def ship(item):
        refs = (
            (notes.at[0], notes.at[1]),
            (pool.at[0, 0, ALL], pool.at[0, 1, ALL]),
            (tight.at[0], tight.at[1]),
            (edge.at[0], edge.at[1]),
        )[item]
        return remote(*refs, ship_send.at[item], ship_recv.at[item], (z, shadow))

    def rim_to_sibling(layer):
        return remote(
            pool.at[layer, 1, NEAR],
            pool.at[layer, 0, FAR],
            rim_send.at[layer, 0],
            rim_recv.at[layer, 0],
            (z, sibling),
        )

    def rim_to_far(layer):
        return remote(
            pool.at[layer, 1, NEAR],
            pool.at[layer, 1, FAR],
            rim_send.at[layer, 1],
            rim_recv.at[layer, 1],
            (z, far_to),
        )

    def direct(there):
        return remote(
            weights.at[z, piece],
            weights.at[z, piece],
            direct_send.at[there],
            direct_recv.at[z],
            (there, p),
        )

    def wants(there):
        return (there != z) & (there + 1 - lax.rem(there, 2) >= z)

    def share(layer, member):
        return remote(
            weights.at[layer, piece],
            weights.at[layer, piece],
            share_send.at[layer, member],
            share_recv.at[layer, piece],
            (z, others[member][0]),
        )

    def pass_on(layer):
        @pl.when((layer < layers) & (layer != z))
        def _():
            remote(
                weights.at[layer, piece],
                weights.at[layer, piece],
                direct_send.at[layer],
                direct_recv.at[layer],
                (pair, p),
            ).wait_recv()
            for member in range(PIECES - 1):
                share(layer, member).start()

    def have_weight(layer):
        @pl.when(layer != z)
        def _():
            for member in range(PIECES - 1):
                index = others[member][1]
                remote(
                    weights.at[layer, piece],
                    weights.at[layer, index],
                    share_send.at[layer, member],
                    share_recv.at[layer, index],
                    (z, sibling),
                ).wait_recv()

    def out_local():
        return pltpu.make_async_copy(pool.at[z + 1, 0, ALL], out_ref.at[0, span], out_send.at[0])

    def out_remote():
        return remote(
            pool.at[pair + 1, 0, ALL],
            out_ref.at[0, span],
            out_send.at[1],
            out_recv.at[0],
            (pair, p),
        )

    def out_arrival():
        return remote(
            pool.at[pair + 1, 0, ALL],
            out_ref.at[0, 1 - span],
            out_send.at[1],
            out_recv.at[0],
            (pair, p),
        )

    pool[0, 0, ALL] = initial_ref[span]
    weights[z] = weight_ref[0].reshape(PIECES, PIECE, WIDTH)
    wanted = jnp.where(span == 0, rows_ref[0:1, :], rows_ref[1:2, :])
    live = lax.broadcasted_iota(jnp.int32, (1, RIM), 1) < count_ref[span, 0]
    notes[0, 16:17, :] = jnp.where(live, wanted, -1).astype(jnp.float32)
    for block in range(OWN):
        first = sources_ref[span, 3 * block]
        second = sources_ref[span, 3 * block + 1]
        third = sources_ref[span, 3 * block + 2]
        at_before = jnp.where(second == OWN, 1, 0) + jnp.where(third == OWN, 2, 0)
        at_after = jnp.where(second == OWN + 1, 1, 0) + jnp.where(third == OWN + 1, 2, 0)
        at_own = jnp.minimum(3 - at_before - at_after, 2)
        own_tile = first + second + third - (2 * OWN + 1)
        place = pl.ds(block * TILE, TILE)
        at_far = jnp.where(core == 1, at_before, at_after)
        at_near = jnp.where(core == 1, at_after, at_before)
        edge[0, place, 0:RIM] = adjacency_ref[span, 3 * block + at_far]
        edge[0, place, RIM : 2 * RIM] = adjacency_ref[span, 3 * block + at_near]
        tight[0, place] = adjacency_ref[span, 3 * block + at_own]
        for t in range(OWN):
            chosen = jnp.where(own_tile == t, 1.0, 0.0)
            notes[0, 4 * block + t : 4 * block + t + 1, :] = jnp.full((1, TILE), chosen)

    lane = lax.broadcasted_iota(jnp.int32, (RIM, TILE), 1).astype(jnp.float32)

    def picker(unit):
        turned = jnp.broadcast_to(notes[unit, 16:17, :], (RIM, RIM)).T
        return jnp.concatenate(
            [jnp.where(turned == lane + float(t * TILE), 1.0, 0.0) for t in range(OWN)], axis=1
        ).astype(jnp.bfloat16)

    def first_rim(unit):
        pool[0, 1 - unit, NEAR] = dot(picker(unit), pool[0, unit, ALL]).astype(jnp.bfloat16)

    def spread(unit):
        pick = picker(unit)
        for block in range(OWN):
            place = pl.ds(block * TILE, TILE)
            own = tight[unit, place].astype(jnp.float32)
            for t in range(OWN):
                mask = notes[unit, 4 * block + t : 4 * block + t + 1, :]
                wide[unit, place, t * TILE : (t + 1) * TILE] = (own * mask).astype(jnp.bfloat16)
        rim_wide[unit] = dot(pick, wide[unit]).astype(jnp.bfloat16)
        rim_edge[unit] = dot(pick, edge[unit]).astype(jnp.bfloat16)

    def start_rim(unit, layer):
        early[unit] = dot(rim_wide[unit], pool[layer, unit, ALL])

    def finish(aggregate, anchor, layer):
        mixing = betas_ref[layer]
        blended = (1.0 - alpha_mix) * aggregate + alpha_mix * anchor.astype(jnp.float32)
        projected = dot(blended.astype(jnp.bfloat16), weights[layer].reshape(WIDTH, WIDTH))
        return jnp.maximum((1.0 - mixing) * blended + mixing * projected, 0.0).astype(jnp.bfloat16)

    def end_rim(unit, layer):
        aggregate = early[unit] + dot(rim_edge[unit], pool[layer, unit, EDGES])
        pool[layer + 1, 1 - unit, NEAR] = finish(aggregate, pool[0, 1 - unit, NEAR], layer)

    def all_rows(unit, layer):
        aggregate = dot(wide[unit], pool[layer, unit, ALL])
        aggregate += dot(edge[unit], pool[layer, unit, EDGES])
        pool[layer + 1, unit, ALL] = finish(aggregate, pool[0, unit, ALL], layer)

    first_rim(0)
    spread(0)
    pl.semaphore_wait(barrier, 6 + sections - 1)
    for item in range(4):
        ship(item).start()
    rim_to_sibling(0).start()
    rim_to_far(0).start()

    def send_weight(step, carry):
        there = sections - 1 - step

        @pl.when(wants(there))
        def _():
            direct(there).start()

        return carry

    lax.fori_loop(0, sections, send_weight, 0)

    start_rim(0, 0)
    ship(0).wait_recv()
    ship(1).wait_recv()
    first_rim(1)
    for layer in range(AHEAD):
        pass_on(layer)
    have_weight(0)
    rim_to_sibling(0).wait_recv()
    end_rim(0, 0)
    rim_to_sibling(1).start()

    @pl.when(layers > 2)
    def _():
        rim_to_far(1).start()

    all_rows(0, 0)
    start_rim(0, 1)
    ship(2).wait_recv()
    ship(3).wait_recv()
    spread(1)
    start_rim(1, 0)

    def step(i, carry):
        last = i == layers - 2

        @pl.when(last & (span == 0))
        def _():
            out_local().start()

        @pl.when(last & (span == 1))
        def _():
            out_remote().start()

        rim_to_far(i).wait_recv()
        end_rim(1, i)
        have_weight(i + 1)
        rim_to_sibling(i + 1).wait_recv()

        @pl.when(i < layers - 2)
        def _():
            end_rim(0, i + 1)
            rim_to_sibling(i + 2).start()

            @pl.when(i < layers - 3)
            def _():
                rim_to_far(i + 2).start()

            pass_on(i + AHEAD)
            all_rows(1, i)
            start_rim(1, i + 1)

        all_rows(0, i + 1)

        @pl.when(i < layers - 2)
        def _():
            start_rim(0, i + 2)

        return carry

    lax.fori_loop(0, layers - 1, step, 0)

    @pl.when(span == 1)
    def _():
        out_local().start()

    @pl.when(span == 0)
    def _():
        out_remote().start()

    for item in range(4):
        ship(item).wait_send()

    def sent(layer, carry):
        rim_to_sibling(layer).wait_send()

        @pl.when(layer < layers - 1)
        def _():
            rim_to_far(layer).wait_send()

        @pl.when(layer != z)
        def _():
            for member in range(PIECES - 1):
                share(layer, member).wait_send()

        return carry

    lax.fori_loop(0, layers, sent, 0)

    def sent_weight(there, carry):
        @pl.when(wants(there))
        def _():
            direct(there).wait_send()

        return carry

    lax.fori_loop(0, sections, sent_weight, 0)
    out_local().wait()
    out_remote().wait_send()
    out_arrival().wait_recv()


def solution(mesh):
    sections, shards = mesh.shape["section"], mesh.shape["node"]
    row_shards = 8 if shards >= 32 else 2
    ordinals = np.arange(sections, dtype=np.float32)
    betas = np.log(np.float32(lambda_decay) / (ordinals + np.float32(1.0)) + np.float32(1.0))

    def on_device(initial, adjacency, sources, boundary_rows, boundary_count, layer_weights):
        def body(*refs):
            layers_kernel(sections, shards, row_shards, *refs)

        smem = pl.BlockSpec(memory_space=pltpu.SMEM)
        vmem = pl.BlockSpec(memory_space=pltpu.VMEM)
        dma = pltpu.SemaphoreType.DMA
        return pl.pallas_call(
            body,
            out_shape=jax.ShapeDtypeStruct((1, SPANS, ROWS, WIDTH), jnp.bfloat16),
            in_specs=[smem, smem, smem, vmem, vmem, vmem, vmem],
            out_specs=pl.BlockSpec(memory_space=pl.ANY),
            scratch_shapes=[
                pltpu.VMEM((sections, PIECES, PIECE, WIDTH), jnp.bfloat16),
                pltpu.VMEM((sections + 1, 2, POOL, WIDTH), jnp.bfloat16),
                pltpu.VMEM((2, ROWS, ROWS), jnp.bfloat16),
                pltpu.VMEM((2, ROWS, 2 * RIM), jnp.bfloat16),
                pltpu.VMEM((2, ROWS, TILE), jnp.bfloat16),
                pltpu.VMEM((2, NOTES, TILE), jnp.float32),
                pltpu.VMEM((2, RIM, ROWS), jnp.bfloat16),
                pltpu.VMEM((2, RIM, 2 * RIM), jnp.bfloat16),
                pltpu.VMEM((2, RIM, WIDTH), jnp.float32),
                dma((4,)),
                dma((4,)),
                dma((sections, 2)),
                dma((sections, 2)),
                dma((sections,)),
                dma((sections,)),
                dma((sections, PIECES - 1)),
                dma((sections, PIECES)),
                dma((2,)),
                dma((1,)),
            ],
            compiler_params=pltpu.CompilerParams(
                collective_id=0, has_side_effects=True, vmem_limit_bytes=48 * 1024 * 1024
            ),
        )(
            jnp.asarray(betas, jnp.float32),
            sources,
            boundary_count,
            boundary_rows,
            initial,
            adjacency,
            layer_weights,
        )

    in_specs = (
        P(None, "node", None),
        P(None, "node", None, None),
        P(None, "node"),
        P(None, "node"),
        P(None, "node"),
        P("section", None, None),
    )
    out_specs = P("section", None, "node", None)
    return jax.shard_map(
        on_device, mesh=mesh, in_specs=in_specs, out_specs=out_specs, check_vma=False
    )
```

time: 605 us -> 83.4 us (0.14); the launches traced: 595 us -> 82.8 us
  waiting for transfers between devices: 264 us -> 0 us
  local copies, waits for them, and re-layouts: 110 us -> 5.33 us
  starting transfers between devices: 96.7 us -> 0 us
  other arithmetic: 78.8 us -> 0 us
  Pallas kernels: 0 us -> 77.4 us
  matrix products: 43.1 us -> 0 us
    ppermute x48 -> x0, waiting for transfers between devices: 264 us -> none  [the longest x16 172 us: from_behind(): return lax.ppermute(x, axis, pairs)]
    ppermute x48 -> x0, starting transfers between devices: 96.7 us -> none  [the longest x16 39 us: extended_2(): lax.ppermute(head, axis, [((i + 1) % count, i) for i in range(count)])]
    pallas_call x0 -> x1, Pallas kernels: none -> 77.4 us  [on_device(): pl.pallas_call(body, out_shape=jax.ShapeDtypeStruct((1, SPANS, ROWS, WIDT...]
    gather x64 -> x0, local copies, waits for them, and re-layouts: 64.3 us -> none  [the longest x48 37.7 us: gcn_layer(): picked = jnp.take_along_axis(source_pool, sources[:, :, None, None], axis=1)]
    dot_general x32 -> x0, matrix products: 43.1 us -> none  [the longest x16 35.5 us: gcn_layer(): jnp.einsum('cntk,cnkd->cntd', adjacency, picked, preferred_element_type=j...]
    convert_element_type x32 -> x0, other arithmetic: 39.7 us -> none  [the longest x16 27.4 us: finish_rows(): blended.astype(jnp.bfloat16).reshape(count_spans * row_count, width)]
    mul x32 -> x0, local copies, waits for them, and re-layouts: 26.3 us -> none  [the longest x16 21 us: finish_rows(): alpha_mix * anchor.astype(jnp.float32)]
    reduce_sum x16 -> x0, other arithmetic: 20 us -> none  [gcn_layer(): aggregate = products.reshape(count_spans, row_count // tile_size, per_row...]
  transfers between devices with their start and end apart: 48 -> 0, of which waited for: 32 -> 0; matrix products, arithmetic and copies ran while one was open for 4% -> 0% of each run, Pallas kernels for 0% -> 0%
where the time goes in v2:
time: 83.4 us; the launch traced here: 82.8 us
  Pallas kernels  77.4 us (93%)
  local copies, waits for them, and re-layouts  5.33 us (6%)
    pallas_call x1, Pallas kernels, on_device(): pl.pallas_call(body, out_shape=jax.ShapeDtypeStruct((1, SPANS, ROWS, WIDT...  77.4 us
    unnamed x14, local copies, waits for them, and re-layouts  5.33 us

profile of v2, /device:TPU:480, one launch (start us, length us, event | category | flops | bytes accessed | tf_op | source)
XLA Modules:
  0.0 82.8 jit_solution(4894202202423180285)
XLA Ops:
  0.0 0.0 copy-start.5
  0.0 0.0 copy-start.3
  0.0 0.8 copy.8.refs_2_
  0.8 0.0 copy-done.5
  0.8 0.0 copy-done.3
  0.8 0.0 copy-start
  0.8 1.1 %copy-done = bf16[2,12,128,128]{3,2,1,0:T(8,128)(2,1)S(1)} copy-done((bf16[2,12,128,128]{3,2,1,0:T(8,128)(2,1)S(1)}, bf16[2,12,128,128]{3,2,1,0:T(8,128)(2,1)}, u32[]{:S(2)}) %copy-start) | copy-done | bytes 786456
  1.9 0.0 copy-start.1
  1.9 1.0 %copy-done.1 = bf16[2,512,256]{2,1,0:T(8,128)(2,1)S(1)} copy-done((bf16[2,512,256]{2,1,0:T(8,128)(2,1)S(1)}, bf16[2,512,256]{2,1,0:T(8,128)(2,1)}, u32[]{:S(2)}) %copy-start.1) | copy-done | bytes 524312
  3.0 0.0 copy-start.2
  3.0 0.9 %copy-done.2 = bf16[1,256,256]{2,1,0:T(8,128)(2,1)S(1)} copy-done((bf16[1,256,256]{2,1,0:T(8,128)(2,1)S(1)}, bf16[1,256,256]{2,1,0:T(8,128)(2,1)}, u32[]{:S(2)}) %copy-start.2) | copy-done | bytes 131096
  3.9 0.0 copy-start.4
  3.9 0.7 copy-done.4
  4.5 77.4 %shard_map.73 = bf16[1,2,512,256]{3,2,1,0:T(8,128)(2,1)S(1)} custom-call(f32[16]{0:T(128)S(1)} %copy-done.5, s32[2,12]{1,0:T(2,128)S(1)} %copy-done.3, s32[2,1]{1,0:T(2,128)S(1)} %copy.8.refs_2_, s32[2,128]{1,0:T(2,128)S(1)} %copy-done.4, bf16[2,512,256]{2,1,0:T(8,128)(2,1)S(1)} %copy-done.1, bf16[2,12,128,128]{3,2,1,0:T(8,128)(2,1)S(1)} %copy-done, ...), custom_call_target="tpu_custom_call" | custom-call | tf_op jit(solution)/shard_map/pallas_call | solution.py:400
  82.0 0.8 copy.10
Async XLA Ops:
  0.0 0.8 copy-start.5
  0.0 0.8 copy-start.3
  0.8 1.1 %copy-start = (bf16[2,12,128,128]{3,2,1,0:T(8,128)(2,1)S(1)}, bf16[2,12,128,128]{3,2,1,0:T(8,128)(2,1)}, u32[]{:S(2)}) copy-start(bf16[2,12,128,128]{3,2,1,0:T(8,128)(2,1)} %refs_5_.1) | copy-start | bytes 2359300
  1.9 1.0 %copy-start.1 = (bf16[2,512,256]{2,1,0:T(8,128)(2,1)S(1)}, bf16[2,512,256]{2,1,0:T(8,128)(2,1)}, u32[]{:S(2)}) copy-start(bf16[2,512,256]{2,1,0:T(8,128)(2,1)} %refs_4_.1) | copy-start | bytes 1572868
  3.0 0.9 %copy-start.2 = (bf16[1,256,256]{2,1,0:T(8,128)(2,1)S(1)}, bf16[1,256,256]{2,1,0:T(8,128)(2,1)}, u32[]{:S(2)}) copy-start(bf16[1,256,256]{2,1,0:T(8,128)(2,1)} %refs_6_.1) | copy-start | bytes 393220
  3.9 0.7 copy-start.4

commit v3 on v2

v3 whole, which is shorter than its diff:
```python
import jax
import jax.numpy as jnp
import numpy as np
from jax import lax
from jax.experimental import pallas as pl
from jax.experimental.pallas import tpu as pltpu
from jax.sharding import PartitionSpec as P

MESH = pl.DeviceIdType.MESH

alpha_mix = 0.1
lambda_decay = 0.5

SPANS = 2
ROWS = 512
TILE = 128
WIDTH = 256
RIM = 128
OWN = ROWS // TILE
POOL = ROWS + 2 * RIM
PARTS = 2
PART = WIDTH // PARTS
NOTES = 24

ALL = pl.ds(0, ROWS)
FAR = pl.ds(ROWS, RIM)
NEAR = pl.ds(ROWS + RIM, RIM)
EDGES = pl.ds(ROWS, 2 * RIM)


def dot(a, b):
    return jnp.dot(a, b, preferred_element_type=jnp.float32)


def layers_kernel(
    sections,
    shards,
    initial_ref,
    adjacency_ref,
    sources_ref,
    rows_ref,
    count_ref,
    weight_ref,
    out_ref,
    betas,
    tiles,
    sources,
    rows,
    count,
    weights,
    pool,
    wide,
    edge,
    tight,
    notes,
    rim_wide,
    rim_edge,
    early,
    ship_send,
    ship_recv,
    rim_send,
    rim_recv,
    near_send,
    near_recv,
    down_send,
    down_recv,
    up_send,
    up_recv,
    side_send,
    side_recv,
    out_send,
    out_recv,
    in_sem,
):
    z = lax.axis_index("section")
    p = lax.axis_index("node")
    span = lax.rem(z, 2)
    core = lax.rem(p, 2)
    shadow = lax.rem(p - 1 + 2 * core + shards, shards)
    sibling = p + 1 - 2 * core
    far_to = lax.rem(p + 2 - 4 * core + shards, shards)
    far_from = lax.rem(p - 2 + 4 * core + shards, shards)
    below, above = lax.rem(z + sections - 1, sections), lax.rem(z + 1, sections)
    pair = z + 1 - 2 * span
    layers = z + 2 - span
    down_steps = sections // 2
    up_steps = sections - 1 - down_steps

    barrier = pltpu.get_barrier_semaphore()
    greeted = [(z, node) for node in (sibling, far_to, far_from, shadow)]
    greeted += [(below, p), (above, p)]
    for device in greeted:
        pl.semaphore_signal(barrier, inc=1, device_id=device, device_id_type=MESH)

    inputs = [
        pltpu.make_async_copy(src, dst, in_sem.at[index])
        for index, (src, dst) in enumerate(
            (
                (sources_ref, sources),
                (count_ref, count),
                (rows_ref, rows),
                (initial_ref.at[span], pool.at[0, 0, ALL]),
                (adjacency_ref.at[span], tiles),
                (weight_ref.at[0], weights.at[z]),
            )
        )
    ]
    for copy in inputs:
        copy.start()

    def remote(src, dst, send, recv, device):
        return pltpu.make_async_remote_copy(
            src_ref=src,
            dst_ref=dst,
            send_sem=send,
            recv_sem=recv,
            device_id=device,
            device_id_type=MESH,
        )

    def ship(item):
        refs = (
            (notes.at[0], notes.at[1]),
            (pool.at[0, 0, ALL], pool.at[0, 1, ALL]),
            (tight.at[0], tight.at[1]),
            (edge.at[0], edge.at[1]),
        )[item]
        return remote(*refs, ship_send.at[item], ship_recv.at[item], (z, shadow))

    def rim_to_sibling(layer):
        return remote(
            pool.at[layer, 1, NEAR],
            pool.at[layer, 0, FAR],
            rim_send.at[layer, 0],
            rim_recv.at[layer, 0],
            (z, sibling),
        )

    def rim_to_far(layer):
        return remote(
            pool.at[layer, 1, NEAR],
            pool.at[layer, 1, FAR],
            rim_send.at[layer, 1],
            rim_recv.at[layer, 1],
            (z, far_to),
        )

    def rim_to_near(layer):
        return remote(
            pool.at[layer, 1, NEAR],
            pool.at[layer, 0, NEAR],
            near_send.at[layer],
            near_recv.at[layer],
            (z, shadow),
        )

    def part_of(layer, part):
        return weights.at[layer, pl.ds(part * PART, PART)]

    def down_copy(step, part):
        ref = part_of(lax.rem(z + step - 1, sections), part)
        at = (step - 1, part)
        return remote(ref, ref, down_send.at[at], down_recv.at[at], (below, p))

    def down_arrival(step, part):
        ref = part_of(lax.rem(z + step, sections), part)
        at = (step - 1, part)
        return remote(ref, ref, down_send.at[at], down_recv.at[at], (below, p))

    def up_copy(step, part):
        ref = part_of(lax.rem(z - step + 1 + sections, sections), part)
        at = (step - 1, part)
        return remote(ref, ref, up_send.at[at], up_recv.at[at], (above, p))

    def up_arrival(step, part):
        ref = part_of(lax.rem(z - step + sections, sections), part)
        at = (step - 1, part)
        return remote(ref, ref, up_send.at[at], up_recv.at[at], (above, p))

    def sends_up(step):
        return (step <= up_steps) & (step <= z + 1) & (z < sections - 1)

    def to_side(layer, part):
        ref = part_of(layer, part)
        return remote(
            ref, ref, side_send.at[layer, part], side_recv.at[layer, part], (z, sibling)
        )

    def relay_down(step):
        @pl.when((core == 1) & (step <= down_steps))
        def _():
            layer = lax.rem(z + step, sections)
            for part in range(PARTS):
                down_arrival(step, part).wait_recv()

                @pl.when(step < down_steps)
                def _():
                    down_copy(step + 1, part).start()

                @pl.when(layer < layers)
                def _():
                    to_side(layer, part).start()

    def relay_up(step):
        @pl.when((core == 1) & (step <= up_steps) & (step <= z))
        def _():
            for part in range(PARTS):
                up_arrival(step, part).wait_recv()

                @pl.when(sends_up(step + 1))
                def _():
                    up_copy(step + 1, part).start()

                to_side(z - step, part).start()

    def have_weight(layer):
        @pl.when((core == 0) & (layer != z))
        def _():
            for part in range(PARTS):
                to_side(layer, part).wait_recv()

    def out_local():
        return pltpu.make_async_copy(pool.at[z + 1, 0, ALL], out_ref.at[0, span], out_send.at[0])

    def out_remote(half):
        return remote(
            pool.at[pair + 1, 0, ALL],
            out_ref.at[0, half],
            out_send.at[1],
            out_recv.at[0],
            (pair, p),
        )

    ordinals = np.arange(sections, dtype=np.float32)
    mixings = np.log(np.float32(lambda_decay) / (ordinals + np.float32(1.0)) + np.float32(1.0))
    for layer in range(sections):
        betas[layer] = jnp.float32(mixings[layer])
    for copy in inputs[:3]:
        copy.wait()
    wanted = jnp.where(span == 0, rows[0:1, :], rows[1:2, :])
    live = lax.broadcasted_iota(jnp.int32, (1, RIM), 1) < count[0, span]
    notes[0, 16:17, :] = jnp.where(live, wanted, -1).astype(jnp.float32)
    inputs[4].wait()
    for block in range(OWN):
        first = sources[span, 3 * block]
        second = sources[span, 3 * block + 1]
        third = sources[span, 3 * block + 2]
        at_before = jnp.where(second == OWN, 1, 0) + jnp.where(third == OWN, 2, 0)
        at_after = jnp.where(second == OWN + 1, 1, 0) + jnp.where(third == OWN + 1, 2, 0)
        at_own = jnp.minimum(3 - at_before - at_after, 2)
        own_tile = first + second + third - (2 * OWN + 1)
        place = pl.ds(block * TILE, TILE)
        at_far = jnp.where(core == 1, at_before, at_after)
        at_near = jnp.where(core == 1, at_after, at_before)
        edge[0, place, 0:RIM] = tiles[3 * block + at_far]
        edge[0, place, RIM : 2 * RIM] = tiles[3 * block + at_near]
        tight[0, place] = tiles[3 * block + at_own]
        for t in range(OWN):
            chosen = jnp.where(own_tile == t, 1.0, 0.0)
            notes[0, 4 * block + t : 4 * block + t + 1, :] = jnp.full((1, TILE), chosen)

    lane = lax.broadcasted_iota(jnp.int32, (RIM, TILE), 1).astype(jnp.float32)

    def picker(unit):
        turned = jnp.broadcast_to(notes[unit, 16:17, :], (RIM, RIM)).T
        return jnp.concatenate(
            [jnp.where(turned == lane + float(t * TILE), 1.0, 0.0) for t in range(OWN)], axis=1
        ).astype(jnp.bfloat16)

    def first_rim(unit):
        pool[0, 1 - unit, NEAR] = dot(picker(unit), pool[0, unit, ALL]).astype(jnp.bfloat16)

    def spread(unit):
        pick = picker(unit)
        for block in range(OWN):
            place = pl.ds(block * TILE, TILE)
            own = tight[unit, place].astype(jnp.float32)
            for t in range(OWN):
                mask = notes[unit, 4 * block + t : 4 * block + t + 1, :]
                wide[unit, place, t * TILE : (t + 1) * TILE] = (own * mask).astype(jnp.bfloat16)
        rim_wide[unit] = dot(pick, wide[unit]).astype(jnp.bfloat16)
        rim_edge[unit] = dot(pick, edge[unit]).astype(jnp.bfloat16)

    def start_rim(unit, layer):
        early[unit] = dot(rim_wide[unit], pool[layer, unit, ALL])

    def finish(aggregate, anchor, layer):
        mixing = betas[layer]
        blended = (1.0 - alpha_mix) * aggregate + alpha_mix * anchor.astype(jnp.float32)
        projected = dot(blended.astype(jnp.bfloat16), weights[layer])
        return jnp.maximum((1.0 - mixing) * blended + mixing * projected, 0.0).astype(jnp.bfloat16)

    def end_rim(unit, layer):
        aggregate = early[unit] + dot(rim_edge[unit], pool[layer, unit, EDGES])
        pool[layer + 1, 1 - unit, NEAR] = finish(aggregate, pool[0, 1 - unit, NEAR], layer)

    def all_rows(unit, layer):
        aggregate = dot(wide[unit], pool[layer, unit, ALL])
        aggregate += dot(edge[unit], pool[layer, unit, EDGES])
        pool[layer + 1, unit, ALL] = finish(aggregate, pool[0, unit, ALL], layer)

    inputs[3].wait()
    first_rim(0)
    spread(0)
    inputs[5].wait()
    pl.semaphore_wait(barrier, len(greeted))
    for copy in (rim_to_sibling(0), rim_to_near(0), rim_to_far(0)):
        copy.start()

    @pl.when(core == 1)
    def _():
        for part in range(PARTS):
            down_copy(1, part).start()

            @pl.when(sends_up(1))
            def _():
                up_copy(1, part).start()

    for item in (0, 2, 3, 1):
        ship(item).start()
    start_rim(0, 0)

    down_first = jnp.minimum(sections + 1 - z, down_steps)
    up_first = jnp.minimum(sections - z, up_steps)

    def relay(step, carry):
        @pl.when(step <= down_first)
        def _():
            relay_down(step)

        @pl.when(step <= up_first)
        def _():
            relay_up(step)

        return carry

    lax.fori_loop(1, down_steps + 1, relay, 0)
    have_weight(0)
    rim_to_sibling(0).wait_recv()
    rim_to_near(0).wait_recv()
    end_rim(0, 0)
    rim_to_sibling(1).start()
    rim_to_near(1).start()

    @pl.when(layers > 2)
    def _():
        rim_to_far(1).start()

    all_rows(0, 0)
    start_rim(0, 1)
    relay_down(down_first + 1)
    have_weight(1)
    rim_to_sibling(1).wait_recv()
    rim_to_near(1).wait_recv()

    @pl.when(layers > 2)
    def _():
        end_rim(0, 1)
        rim_to_sibling(2).start()

        @pl.when(layers > 3)
        def _():
            rim_to_far(2).start()

    all_rows(0, 1)
    relay_down(down_first + 2)
    ship(0).wait_recv()
    ship(2).wait_recv()
    ship(3).wait_recv()
    spread(1)
    ship(1).wait_recv()
    rim_to_far(0).wait_recv()

    @pl.when(layers > 2)
    def _():
        start_rim(0, 2)
        all_rows(1, 0)
        start_rim(1, 1)

    def first_out():
        @pl.when(span == 0)
        def _():
            out_local().start()

        @pl.when(span == 1)
        def _():
            out_remote(span).start()

    def step(i, carry):
        @pl.when(i == layers - 2)
        def _():
            first_out()

        rim_to_far(i).wait_recv()
        end_rim(1, i)
        have_weight(i + 1)
        rim_to_sibling(i + 1).wait_recv()

        @pl.when(i < layers - 2)
        def _():
            end_rim(0, i + 1)
            rim_to_sibling(i + 2).start()

            @pl.when(i < layers - 3)
            def _():
                rim_to_far(i + 2).start()

            relay_down(down_first + 2 + i)
            relay_up(up_first + i)
            all_rows(1, i)
            start_rim(1, i + 1)

        all_rows(0, i + 1)

        @pl.when(i < layers - 2)
        def _():
            start_rim(0, i + 2)

        return carry

    lax.fori_loop(1, layers - 1, step, 0)

    @pl.when(layers == 2)
    def _():
        first_out()

    @pl.when(span == 1)
    def _():
        out_local().start()

    @pl.when(span == 0)
    def _():
        out_remote(span).start()

    for item in range(4):
        ship(item).wait_send()
    for layer in range(2):
        rim_to_near(layer).wait_send()

    def sent(layer, carry):
        rim_to_sibling(layer).wait_send()

        @pl.when(layer < layers - 1)
        def _():
            rim_to_far(layer).wait_send()

        @pl.when((core == 1) & (layer != z))
        def _():
            for part in range(PARTS):
                to_side(layer, part).wait_send()

        return carry

    lax.fori_loop(0, layers, sent, 0)

    @pl.when(core == 1)
    def _():
        for part in range(PARTS):
            for step in range(1, down_steps + 1):
                down_copy(step, part).wait_send()
            for step in range(1, up_steps + 1):

                @pl.when(sends_up(step))
                def _():
                    up_copy(step, part).wait_send()

    out_local().wait()
    out_remote(span).wait_send()
    out_remote(1 - span).wait_recv()


def solution(mesh):
    sections, shards = mesh.shape["section"], mesh.shape["node"]

    def on_device(initial, adjacency, sources, boundary_rows, boundary_count, layer_weights):
        def body(*refs):
            layers_kernel(sections, shards, *refs)

        dma = pltpu.SemaphoreType.DMA
        down_steps = sections // 2
        return pl.pallas_call(
            body,
            out_shape=jax.ShapeDtypeStruct((1, SPANS, ROWS, WIDTH), jnp.bfloat16),
            in_specs=[pl.BlockSpec(memory_space=pltpu.HBM)] * 6,
            out_specs=pl.BlockSpec(memory_space=pltpu.HBM),
            scratch_shapes=[
                pltpu.SMEM((sections,), jnp.float32),
                pltpu.VMEM((OWN * 3, TILE, TILE), jnp.bfloat16),
                pltpu.SMEM((SPANS, OWN * 3), jnp.int32),
                pltpu.VMEM((SPANS, RIM), jnp.int32),
                pltpu.SMEM((1, SPANS), jnp.int32),
                pltpu.VMEM((sections, WIDTH, WIDTH), jnp.bfloat16),
                pltpu.VMEM((sections + 1, 2, POOL, WIDTH), jnp.bfloat16),
                pltpu.VMEM((2, ROWS, ROWS), jnp.bfloat16),
                pltpu.VMEM((2, ROWS, 2 * RIM), jnp.bfloat16),
                pltpu.VMEM((2, ROWS, TILE), jnp.bfloat16),
                pltpu.VMEM((2, NOTES, TILE), jnp.float32),
                pltpu.VMEM((2, RIM, ROWS), jnp.bfloat16),
                pltpu.VMEM((2, RIM, 2 * RIM), jnp.bfloat16),
                pltpu.VMEM((2, RIM, WIDTH), jnp.float32),
                dma((4,)),
                dma((4,)),
                dma((sections, 2)),
                dma((sections, 2)),
                dma((2,)),
                dma((2,)),
                dma((down_steps, PARTS)),
                dma((down_steps, PARTS)),
                dma((down_steps, PARTS)),
                dma((down_steps, PARTS)),
                dma((sections, PARTS)),
                dma((sections, PARTS)),
                dma((2,)),
                dma((1,)),
                dma((6,)),
            ],
            compiler_params=pltpu.CompilerParams(
                collective_id=0, has_side_effects=True, vmem_limit_bytes=60 * 1024 * 1024
            ),
        )(
            initial,
            adjacency,
            sources,
            boundary_rows,
            boundary_count.reshape(1, SPANS),
            layer_weights,
        )

    in_specs = (
        P(None, "node", None),
        P(None, "node", None, None),
        P(None, "node"),
        P(None, "node"),
        P(None, "node"),
        P("section", None, None),
    )
    out_specs = P("section", None, "node", None)
    return jax.shard_map(
        on_device, mesh=mesh, in_specs=in_specs, out_specs=out_specs, check_vma=False
    )
```

time: 83.4 us -> 68.3 us (0.82)
  Pallas kernels: 77.4 us -> 66.2 us
  local copies, waits for them, and re-layouts: 5.33 us -> 1.87 us
    pallas_call x1, Pallas kernels: 77.4 us -> 66.2 us  [on_device(): pl.pallas_call(body, out_shape=jax.ShapeDtypeStruct((1, SPANS, ROWS, WIDT...]
    unnamed x14 -> x1, local copies, waits for them, and re-layouts: 5.33 us -> 1.87 us
where the time goes in v3:
time: 68.3 us; the launch traced here: 68.1 us
  Pallas kernels  66.2 us (97%)
  local copies, waits for them, and re-layouts  1.87 us (3%)
    pallas_call x1, Pallas kernels, on_device(): pl.pallas_call(body, out_shape=jax.ShapeDtypeStruct((1, SPANS, ROWS, WIDT...  66.2 us
    unnamed x1, local copies, waits for them, and re-layouts  1.87 us

profile of v3, /device:TPU:480, one launch (start us, length us, event | category | flops | bytes accessed | tf_op | source)
XLA Modules:
  0.0 68.1 jit_solution(12338877348330931609)
XLA Ops:
  0.0 66.2 %shard_map.64 = bf16[1,2,512,256]{3,2,1,0:T(8,128)(2,1)} custom-call(bf16[2,512,256]{2,1,0:T(8,128)(2,1)} %refs_0_.1, bf16[2,12,128,128]{3,2,1,0:T(8,128)(2,1)} %refs_1_.1, s32[2,12]{1,0:T(2,128)} %refs_2_.1, s32[2,128]{1,0:T(2,128)} %refs_3_.1, s32[1,2]{1,0:T(1,128)} %bitcast.1, bf16[1,256,256]{2,1,0:T(8,128)(2,1)} %refs_5_.1), custom_call_target="tpu_custom_call" | custom-call | tf_op jit(solution)/shard_map/pallas_call | solution.py:481
  66.3 1.9 %copy.8 = bf16[1,2,512,256]{3,2,1,0:T(8,128)(2,1)} copy(bf16[1,2,512,256]{3,2,1,0:T(8,128)(2,1)} %shard_map.64) | data formatting | bytes 1048576

commit v4 on v3

--- a/solution.py
+++ b/solution.py
@@ -62,6 +62,7 @@
     rim_recv,
     near_send,
     near_recv,
+    server_send,
     down_send,
     down_recv,
     up_send,
@@ -81,16 +82,22 @@
     far_to = lax.rem(p + 2 - 4 * core + shards, shards)
     far_from = lax.rem(p - 2 + 4 * core + shards, shards)
     below, above = lax.rem(z + sections - 1, sections), lax.rem(z + 1, sections)
-    pair = z + 1 - 2 * span
-    layers = z + 2 - span
-    down_steps = sections // 2
-    up_steps = sections - 1 - down_steps
+    server = z == sections - 2
+    layers = jnp.where(server, sections, jnp.maximum(z + 1, 2))
+    middle = sections // 2
+    up_steps = middle - 1
 
     barrier = pltpu.get_barrier_semaphore()
     greeted = [(z, node) for node in (sibling, far_to, far_from, shadow)]
     greeted += [(below, p), (above, p)]
     for device in greeted:
         pl.semaphore_signal(barrier, inc=1, device_id=device, device_id_type=MESH)
+
+    @pl.when((core == 1) & server)
+    def _():
+        pl.semaphore_signal(barrier, inc=1, device_id=(0, p), device_id_type=MESH)
+
+    greetings = len(greeted) + jnp.where((core == 1) & (z == 0), 1, 0)
 
     inputs = [
         pltpu.make_async_copy(src, dst, in_sem.at[index])
@@ -157,15 +164,37 @@
     def part_of(layer, part):
         return weights.at[layer, pl.ds(part * PART, PART)]
 
-    def down_copy(step, part):
-        ref = part_of(lax.rem(z + step - 1, sections), part)
-        at = (step - 1, part)
-        return remote(ref, ref, down_send.at[at], down_recv.at[at], (below, p))
-
-    def down_arrival(step, part):
-        ref = part_of(lax.rem(z + step, sections), part)
-        at = (step - 1, part)
-        return remote(ref, ref, down_send.at[at], down_recv.at[at], (below, p))
+    def to_below(layer, part):
+        ref = part_of(layer, part)
+        return remote(
+            ref, ref, down_send.at[layer, part], down_recv.at[layer, part], (below, p)
+        )
+
+    def to_server(layer, part):
+        ref = part_of(layer, part)
+        there = (sections - 2, p)
+        return remote(ref, ref, server_send.at[layer, part], down_recv.at[layer, part], there)
+
+    def takes_down(layer):
+        lower = (z < middle) & (layer > z) & (layer < middle)
+        return (core == 1) & (lower | ((z >= middle) & (layer <= z - middle)))
+
+    def sends_below(layer):
+        lower = (z < middle) & (layer >= z) & (layer < middle)
+        upper = (z > middle) & (z < sections - 1) & (layer < z - middle)
+        return (core == 1) & (lower | upper)
+
+    def sends_server(layer):
+        return (core == 1) & (z == 0) & (layer < middle - 1)
+
+    def send_down(layer, part):
+        @pl.when(sends_below(layer))
+        def _():
+            to_below(layer, part).start()
+
+        @pl.when(sends_server(layer))
+        def _():
+            to_server(layer, part).start()
 
     def up_copy(step, part):
         ref = part_of(lax.rem(z - step + 1 + sections, sections), part)
@@ -186,21 +215,24 @@
             ref, ref, side_send.at[layer, part], side_recv.at[layer, part], (z, sibling)
         )
 
-    def relay_down(step):
-        @pl.when((core == 1) & (step <= down_steps))
-        def _():
-            layer = lax.rem(z + step, sections)
+    def relay_down(layer):
+        @pl.when(takes_down(layer))
+        def _():
             for part in range(PARTS):
-                down_arrival(step, part).wait_recv()
-
-                @pl.when(step < down_steps)
-                def _():
-                    down_copy(step + 1, part).start()
+                to_below(layer, part).wait_recv()
+                send_down(layer, part)
 
                 @pl.when(layer < layers)
                 def _():
                     to_side(layer, part).start()
 
+    def take_last():
+        @pl.when((core == 1) & server)
+        def _():
+            for part in range(PARTS):
+                to_below(z + 1, part).wait_recv()
+                to_side(z + 1, part).start()
+
     def relay_up(step):
         @pl.when((core == 1) & (step <= up_steps) & (step <= z))
         def _():
@@ -222,13 +254,14 @@
     def out_local():
         return pltpu.make_async_copy(pool.at[z + 1, 0, ALL], out_ref.at[0, span], out_send.at[0])
 
-    def out_remote(half):
+    def out_below(half):
         return remote(
-            pool.at[pair + 1, 0, ALL],
-            out_ref.at[0, half],
-            out_send.at[1],
-            out_recv.at[0],
-            (pair, p),
+            pool.at[z, 0, ALL], out_ref.at[0, half], out_send.at[1], out_recv.at[0], (below, p)
+        )
+
+    def out_above():
+        return remote(
+            pool.at[z + 2, 0, ALL], out_ref.at[0, span], out_send.at[2], out_recv.at[0], (above, p)
         )
 
     ordinals = np.arange(sections, dtype=np.float32)
@@ -303,14 +336,18 @@
     first_rim(0)
     spread(0)
     inputs[5].wait()
-    pl.semaphore_wait(barrier, len(greeted))
+    pl.semaphore_wait(barrier, greetings)
     for copy in (rim_to_sibling(0), rim_to_near(0), rim_to_far(0)):
         copy.start()
 
     @pl.when(core == 1)
     def _():
         for part in range(PARTS):
-            down_copy(1, part).start()
+            send_down(z, part)
+
+            @pl.when(z == sections - 1)
+            def _():
+                to_below(z, part).start()
 
             @pl.when(sends_up(1))
             def _():
@@ -320,13 +357,17 @@
         ship(item).start()
     start_rim(0, 0)
 
-    down_first = jnp.minimum(sections + 1 - z, down_steps)
+    def relay_down_upper(layer):
+        @pl.when(z >= middle)
+        def _():
+            relay_down(layer)
+
     up_first = jnp.minimum(sections - z, up_steps)
 
     def relay(step, carry):
-        @pl.when(step <= down_first)
-        def _():
-            relay_down(step)
+        @pl.when(z < middle)
+        def _():
+            relay_down(z + step)
 
         @pl.when(step <= up_first)
         def _():
@@ -334,7 +375,8 @@
 
         return carry
 
-    lax.fori_loop(1, down_steps + 1, relay, 0)
+    lax.fori_loop(1, middle, relay, 0)
+    relay_down_upper(0)
     have_weight(0)
     rim_to_sibling(0).wait_recv()
     rim_to_near(0).wait_recv()
@@ -348,7 +390,8 @@
 
     all_rows(0, 0)
     start_rim(0, 1)
-    relay_down(down_first + 1)
+    relay_down_upper(1)
+    take_last()
     have_weight(1)
     rim_to_sibling(1).wait_recv()
     rim_to_near(1).wait_recv()
@@ -363,7 +406,7 @@
             rim_to_far(2).start()
 
     all_rows(0, 1)
-    relay_down(down_first + 2)
+    relay_down_upper(2)
     ship(0).wait_recv()
     ship(2).wait_recv()
     ship(3).wait_recv()
@@ -377,19 +420,14 @@
         all_rows(1, 0)
         start_rim(1, 1)
 
-    def first_out():
-        @pl.when(span == 0)
+    def step(i, carry):
+        @pl.when(i == z - 1)
+        def _():
+            out_below(span).start()
+
+        @pl.when(i == z)
         def _():
             out_local().start()
-
-        @pl.when(span == 1)
-        def _():
-            out_remote(span).start()
-
-    def step(i, carry):
-        @pl.when(i == layers - 2)
-        def _():
-            first_out()
 
         rim_to_far(i).wait_recv()
         end_rim(1, i)
@@ -399,16 +437,17 @@
         @pl.when(i < layers - 2)
         def _():
             end_rim(0, i + 1)
-            rim_to_sibling(i + 2).start()
 
             @pl.when(i < layers - 3)
             def _():
                 rim_to_far(i + 2).start()
 
-            relay_down(down_first + 2 + i)
+            rim_to_sibling(i + 2).start()
+
             relay_up(up_first + i)
             all_rows(1, i)
             start_rim(1, i + 1)
+            relay_down_upper(i + 2)
 
         all_rows(0, i + 1)
 
@@ -420,17 +459,17 @@
 
     lax.fori_loop(1, layers - 1, step, 0)
 
-    @pl.when(layers == 2)
-    def _():
-        first_out()
-
-    @pl.when(span == 1)
+    @pl.when(z == 1)
+    def _():
+        out_below(span).start()
+
+    @pl.when(server)
+    def _():
+        out_above().start()
+
+    @pl.when(jnp.logical_not(server))
     def _():
         out_local().start()
-
-    @pl.when(span == 0)
-    def _():
-        out_remote(span).start()
 
     for item in range(4):
         ship(item).wait_send()
@@ -456,8 +495,20 @@
     @pl.when(core == 1)
     def _():
         for part in range(PARTS):
-            for step in range(1, down_steps + 1):
-                down_copy(step, part).wait_send()
+            for layer in range(middle):
+
+                @pl.when(sends_below(layer))
+                def _():
+                    to_below(layer, part).wait_send()
+
+                @pl.when(sends_server(layer))
+                def _():
+                    to_server(layer, part).wait_send()
+
+            @pl.when(z == sections - 1)
+            def _():
+                to_below(z, part).wait_send()
+
             for step in range(1, up_steps + 1):
 
                 @pl.when(sends_up(step))
@@ -465,8 +516,16 @@
                     up_copy(step, part).wait_send()
 
     out_local().wait()
-    out_remote(span).wait_send()
-    out_remote(1 - span).wait_recv()
+
+    @pl.when(z > 0)
+    def _():
+        out_below(span).wait_send()
+
+    @pl.when(server)
+    def _():
+        out_above().wait_send()
+
+    out_below(1 - span).wait_recv()
 
 
 def solution(mesh):
@@ -477,7 +536,7 @@
             layers_kernel(sections, shards, *refs)
 
         dma = pltpu.SemaphoreType.DMA
-        down_steps = sections // 2
+        middle = sections // 2
         return pl.pallas_call(
             body,
             out_shape=jax.ShapeDtypeStruct((1, SPANS, ROWS, WIDTH), jnp.bfloat16),
@@ -504,13 +563,14 @@
                 dma((sections, 2)),
                 dma((2,)),
                 dma((2,)),
-                dma((down_steps, PARTS)),
-                dma((down_steps, PARTS)),
-                dma((down_steps, PARTS)),
-                dma((down_steps, PARTS)),
+                dma((middle, PARTS)),
                 dma((sections, PARTS)),
                 dma((sections, PARTS)),
-                dma((2,)),
+                dma((middle, PARTS)),
+                dma((middle, PARTS)),
+                dma((sections, PARTS)),
+                dma((sections, PARTS)),
+                dma((3,)),
                 dma((1,)),
                 dma((6,)),
             ],

time: 68.3 us -> 65.1 us (0.953)
  Pallas kernels: 66.2 us -> 63.1 us
    pallas_call x1, Pallas kernels: 66.2 us -> 63.1 us  [on_device(): pl.pallas_call(body, out_shape=jax.ShapeDtypeStruct((1, SPANS, ROWS, WIDT...]
where the time goes in v4:
time: 65.1 us; the launch traced here: 65 us
  Pallas kernels  63.1 us (97%)
  local copies, waits for them, and re-layouts  1.87 us (3%)
    pallas_call x1, Pallas kernels, on_device(): pl.pallas_call(body, out_shape=jax.ShapeDtypeStruct((1, SPANS, ROWS, WIDT...  63.1 us
    unnamed x1, local copies, waits for them, and re-layouts  1.87 us

profile of v4, /device:TPU:480, one launch (start us, length us, event | category | flops | bytes accessed | tf_op | source)
XLA Modules:
  0.0 65.0 jit_solution(4569478050788390819)
XLA Ops:
  0.0 63.1 %shard_map.64 = bf16[1,2,512,256]{3,2,1,0:T(8,128)(2,1)} custom-call(bf16[2,512,256]{2,1,0:T(8,128)(2,1)} %refs_0_.1, bf16[2,12,128,128]{3,2,1,0:T(8,128)(2,1)} %refs_1_.1, s32[2,12]{1,0:T(2,128)} %refs_2_.1, s32[2,128]{1,0:T(2,128)} %refs_3_.1, s32[1,2]{1,0:T(1,128)} %bitcast.1, bf16[1,256,256]{2,1,0:T(8,128)(2,1)} %refs_5_.1), custom_call_target="tpu_custom_call" | custom-call | tf_op jit(solution)/shard_map/pallas_call | solution.py:540
  63.1 1.9 %copy.8 = bf16[1,2,512,256]{3,2,1,0:T(8,128)(2,1)} copy(bf16[1,2,512,256]{3,2,1,0:T(8,128)(2,1)} %shard_map.64) | data formatting | bytes 1048576

commit v5 on v4

--- a/solution.py
+++ b/solution.py
@@ -317,27 +317,41 @@
     def start_rim(unit, layer):
         early[unit] = dot(rim_wide[unit], pool[layer, unit, ALL])
 
-    def finish(aggregate, anchor, layer):
+    def blend(aggregate, anchor):
+        return (1.0 - alpha_mix) * aggregate + alpha_mix * anchor.astype(jnp.float32)
+
+    def finish(blended, blended_b, layer):
         mixing = betas[layer]
-        blended = (1.0 - alpha_mix) * aggregate + alpha_mix * anchor.astype(jnp.float32)
-        projected = dot(blended.astype(jnp.bfloat16), weights[layer])
+        projected = dot(blended_b, weights[layer])
         return jnp.maximum((1.0 - mixing) * blended + mixing * projected, 0.0).astype(jnp.bfloat16)
 
+    def rim_blend(unit, layer):
+        aggregate = early[unit] + dot(rim_edge[unit], pool[layer, unit, EDGES])
+        return blend(aggregate, pool[0, 1 - unit, NEAR])
+
     def end_rim(unit, layer):
-        aggregate = early[unit] + dot(rim_edge[unit], pool[layer, unit, EDGES])
-        pool[layer + 1, 1 - unit, NEAR] = finish(aggregate, pool[0, 1 - unit, NEAR], layer)
+        blended = rim_blend(unit, layer)
+        rim = finish(blended, blended.astype(jnp.bfloat16), layer)
+        pool[layer + 1, 1 - unit, NEAR] = rim
+
+    def end_own_rim(layer):
+        end_rim(0, layer)
+        rim_to_far(layer + 1).start()
+        rim_to_sibling(layer + 1).start()
 
     def all_rows(unit, layer):
         aggregate = dot(wide[unit], pool[layer, unit, ALL])
         aggregate += dot(edge[unit], pool[layer, unit, EDGES])
-        pool[layer + 1, unit, ALL] = finish(aggregate, pool[0, unit, ALL], layer)
+        blended = blend(aggregate, pool[0, unit, ALL])
+        rows_b = blended.astype(jnp.bfloat16)
+        pool[layer + 1, unit, ALL] = finish(blended, rows_b, layer)
 
     inputs[3].wait()
     first_rim(0)
     spread(0)
     inputs[5].wait()
     pl.semaphore_wait(barrier, greetings)
-    for copy in (rim_to_sibling(0), rim_to_near(0), rim_to_far(0)):
+    for copy in (rim_to_far(0), rim_to_near(0), rim_to_sibling(0)):
         copy.start()
 
     @pl.when(core == 1)
@@ -380,14 +394,8 @@
     have_weight(0)
     rim_to_sibling(0).wait_recv()
     rim_to_near(0).wait_recv()
-    end_rim(0, 0)
-    rim_to_sibling(1).start()
+    end_own_rim(0)
     rim_to_near(1).start()
-
-    @pl.when(layers > 2)
-    def _():
-        rim_to_far(1).start()
-
     all_rows(0, 0)
     start_rim(0, 1)
     relay_down_upper(1)
@@ -398,12 +406,7 @@
 
     @pl.when(layers > 2)
     def _():
-        end_rim(0, 1)
-        rim_to_sibling(2).start()
-
-        @pl.when(layers > 3)
-        def _():
-            rim_to_far(2).start()
+        end_own_rim(1)
 
     all_rows(0, 1)
     relay_down_upper(2)
@@ -436,13 +439,7 @@
 
         @pl.when(i < layers - 2)
         def _():
-            end_rim(0, i + 1)
-
-            @pl.when(i < layers - 3)
-            def _():
-                rim_to_far(i + 2).start()
-
-            rim_to_sibling(i + 2).start()
+            end_own_rim(i + 1)
 
             relay_up(up_first + i)
             all_rows(1, i)
@@ -478,10 +475,7 @@
 
     def sent(layer, carry):
         rim_to_sibling(layer).wait_send()
-
-        @pl.when(layer < layers - 1)
-        def _():
-            rim_to_far(layer).wait_send()
+        rim_to_far(layer).wait_send()
 
         @pl.when((core == 1) & (layer != z))
         def _():
@@ -491,6 +485,7 @@
         return carry
 
     lax.fori_loop(0, layers, sent, 0)
+    rim_to_far(layers - 1).wait_recv()
 
     @pl.when(core == 1)
     def _():

time: 65.1 us -> 65.1 us (level)
  no operation moved by 1% of the time
where the time goes in v5:
time: 65.1 us; the launch traced here: 65 us
  Pallas kernels  63.1 us (97%)
  local copies, waits for them, and re-layouts  1.87 us (3%)
    pallas_call x1, Pallas kernels, on_device(): pl.pallas_call(body, out_shape=jax.ShapeDtypeStruct((1, SPANS, ROWS, WIDT...  63.1 us
    unnamed x1, local copies, waits for them, and re-layouts  1.87 us

profile of v5, /device:TPU:480, one launch (start us, length us, event | category | flops | bytes accessed | tf_op | source)
XLA Modules:
  0.0 65.0 jit_solution(1652647553315620608)
XLA Ops:
  0.0 63.1 %shard_map.64 = bf16[1,2,512,256]{3,2,1,0:T(8,128)(2,1)} custom-call(bf16[2,512,256]{2,1,0:T(8,128)(2,1)} %refs_0_.1, bf16[2,12,128,128]{3,2,1,0:T(8,128)(2,1)} %refs_1_.1, s32[2,12]{1,0:T(2,128)} %refs_2_.1, s32[2,128]{1,0:T(2,128)} %refs_3_.1, s32[1,2]{1,0:T(1,128)} %bitcast.1, bf16[1,256,256]{2,1,0:T(8,128)(2,1)} %refs_5_.1), custom_call_target="tpu_custom_call" | custom-call | tf_op jit(solution)/shard_map/pallas_call | solution.py:535
  63.1 1.9 %copy.8 = bf16[1,2,512,256]{3,2,1,0:T(8,128)(2,1)} copy(bf16[1,2,512,256]{3,2,1,0:T(8,128)(2,1)} %shard_map.64) | data formatting | bytes 1048576

commit v6 on v5

--- a/solution.py
+++ b/solution.py
@@ -315,7 +315,10 @@
         rim_edge[unit] = dot(pick, edge[unit]).astype(jnp.bfloat16)
 
     def start_rim(unit, layer):
-        early[unit] = dot(rim_wide[unit], pool[layer, unit, ALL])
+        ready = dot(rim_wide[unit], pool[layer, unit, ALL])
+        if unit == 1:
+            ready += dot(rim_edge[1, :, RIM : 2 * RIM], pool[layer, 1, NEAR])
+        early[unit] = ready
 
     def blend(aggregate, anchor):
         return (1.0 - alpha_mix) * aggregate + alpha_mix * anchor.astype(jnp.float32)
@@ -326,7 +329,11 @@
         return jnp.maximum((1.0 - mixing) * blended + mixing * projected, 0.0).astype(jnp.bfloat16)
 
     def rim_blend(unit, layer):
-        aggregate = early[unit] + dot(rim_edge[unit], pool[layer, unit, EDGES])
+        if unit == 1:
+            late = dot(rim_edge[1, :, 0:RIM], pool[layer, 1, FAR])
+        else:
+            late = dot(rim_edge[0], pool[layer, 0, EDGES])
+        aggregate = early[unit] + late
         return blend(aggregate, pool[0, 1 - unit, NEAR])
 
     def end_rim(unit, layer):

time: 65.1 us -> 65.1 us (level)
  no operation moved by 1% of the time
where the time goes in v6:
time: 65.1 us; the launch traced here: 64.9 us
  Pallas kernels  63 us (97%)
  local copies, waits for them, and re-layouts  1.87 us (3%)
    pallas_call x1, Pallas kernels, on_device(): pl.pallas_call(body, out_shape=jax.ShapeDtypeStruct((1, SPANS, ROWS, WIDT...  63 us
    unnamed x1, local copies, waits for them, and re-layouts  1.87 us

profile of v6, /device:TPU:480, one launch (start us, length us, event | category | flops | bytes accessed | tf_op | source)
XLA Modules:
  0.0 64.9 jit_solution(2030947826097189534)
XLA Ops:
  0.0 63.0 %shard_map.64 = bf16[1,2,512,256]{3,2,1,0:T(8,128)(2,1)} custom-call(bf16[2,512,256]{2,1,0:T(8,128)(2,1)} %refs_0_.1, bf16[2,12,128,128]{3,2,1,0:T(8,128)(2,1)} %refs_1_.1, s32[2,12]{1,0:T(2,128)} %refs_2_.1, s32[2,128]{1,0:T(2,128)} %refs_3_.1, s32[1,2]{1,0:T(1,128)} %bitcast.1, bf16[1,256,256]{2,1,0:T(8,128)(2,1)} %refs_5_.1), custom_call_target="tpu_custom_call" | custom-call | tf_op jit(solution)/shard_map/pallas_call | solution.py:542
  63.0 1.9 %copy.8 = bf16[1,2,512,256]{3,2,1,0:T(8,128)(2,1)} copy(bf16[1,2,512,256]{3,2,1,0:T(8,128)(2,1)} %shard_map.64) | data formatting | bytes 1048576
